TPU v7x, 256 devices: a whole 4x4x8 slice. The times are simulated.
256 devices in a mesh: rows: 64 (over x, z, core), grp: 4 (over y).
Axes of the slice: x: 4, y: 4, z: 8, core: 2. Of those that a mesh axis runs over, the one named last changes fastest.
Arguments:
- table: bfloat16 [524288, 512], P(('rows', 'grp')), may hold values from -30 to 30
- sketch: bfloat16 [512, 256], replicated, may hold values from -0.25 to 0.25
Outputs:
- basis: float32 [524288, 256], P(('rows', 'grp'))
- projection: float32 [256, 512], replicated
All inputs are finite; a program needn't handle non-finite values.
Results may differ from a plain program's by a relative error of at most 0.0004.
Values sent between devices are 32-bit elements; how exact they have to be, the bound alone decides.
No kernel may reach another device: no remote copies, remote signals or barrier semaphores. Data moves between devices by JAX's collectives and lax.ppermute only.
A program may use at most 64 MiB of HBM per device.

v0:
```python
import math

import jax
import jax.numpy as jnp
from jax import lax
from jax.sharding import PartitionSpec as P

SWEEPS = 12


def partner(block, axis, apart):
    count = lax.axis_size(axis)
    route = []
    for low in range(count):
        high = low | 1 << apart
        if high != low and high < count:
            route += [(low, high), (high, low)]
    return lax.ppermute(block, axis, route)


def inverse_root(gram):
    high = lax.Precision.HIGHEST
    eye = jnp.eye(gram.shape[0], dtype=jnp.float32)
    scale = jnp.sqrt(jnp.sum(gram * gram))
    start_y = gram / scale

    def sweep(index, carry):
        cur_y, cur_z = carry
        factor = 1.5 * eye - 0.5 * jnp.dot(cur_z, cur_y, precision=high)
        return (jnp.dot(cur_y, factor, precision=high), jnp.dot(factor, cur_z, precision=high))

    final_y, final_z = lax.fori_loop(0, SWEEPS, sweep, (start_y, eye))
    return final_z / jnp.sqrt(scale)


def merged_gram(local_gram):
    total = local_gram
    for bit_rows in range(lax.axis_size("rows").bit_length() - 1):
        total = total + partner(total, "rows", bit_rows)
    for bit_grp in range(lax.axis_size("grp").bit_length() - 1):
        total = total + partner(total, "grp", bit_grp)
    return total


def on_device(table, sketch):
    high = lax.Precision.HIGHEST
    root = math.sqrt(table.shape[0] * lax.axis_size("rows") * lax.axis_size("grp"))
    wide_table = table.astype(jnp.float32)
    first_range = jnp.dot(table, sketch, preferred_element_type=jnp.float32)
    first_gram = merged_gram(jnp.einsum("rk,rl->kl", first_range, first_range, precision=high))
    first_inverse = inverse_root(first_gram)
    first_basis = jnp.dot(first_range, first_inverse, precision=high)
    local_power = jnp.einsum("rn,rk->nk", wide_table, first_basis, precision=high)
    power = lax.psum(local_power, ("rows", "grp"))
    second_range = jnp.dot(wide_table, power, precision=high)
    second_gram = merged_gram(jnp.einsum("rk,rl->kl", second_range, second_range, precision=high))
    second_inverse = inverse_root(second_gram)
    second_basis = jnp.dot(second_range, second_inverse, precision=high)
    local_coeff = jnp.einsum("rk,rn->kn", second_basis, wide_table, precision=high)
    coeff = lax.psum(local_coeff, ("rows", "grp"))
    return (second_basis * root, coeff / root)


def solution(mesh):
    in_specs = (P(("rows", "grp"), None), P())
    out_specs = (P(("rows", "grp"), None), P())
    return jax.shard_map(
        on_device, mesh=mesh, in_specs=in_specs, out_specs=out_specs, check_vma=False
    )
```

profile of v0, /device:TPU:1, one launch (start us, length us, event | category | flops | bytes accessed | tf_op | source)
XLA Modules:
  0.0 731.7 jit_solution(3437402815008591136)
XLA Ops:
  10.4 3.6 fusion.16
  14.1 3.3 collective-permute-start
  18.7 7.5 %collective-permute-done.1 = f32[256,256]{1,0:T(8,128)S(1)} collective-permute-done((f32[256,256]{1,0:T(8,128)S(1)}, f32[256,256]{1,0:T(8,128)S(1)}, u32[]{:S(2)}, u32[]{:S(2)}) %collective-permute-start.1) | collective-permute-done | bytes 262176 | tf_op jit(solution)/shard_map/ppermute | solution.py:18
  28.0 12.8 %collective-permute-done.2 = f32[256,256]{1,0:T(8,128)S(1)} collective-permute-done((f32[256,256]{1,0:T(8,128)S(1)}, f32[256,256]{1,0:T(8,128)S(1)}, u32[]{:S(2)}, u32[]{:S(2)}) %collective-permute-start.2) | collective-permute-done | bytes 262176 | tf_op jit(solution)/shard_map/ppermute | solution.py:18
  40.8 5.1 collective-permute-start.3
  45.9 11.6 %collective-permute-done.3 = f32[256,256]{1,0:T(8,128)S(1)} collective-permute-done((f32[256,256]{1,0:T(8,128)S(1)}, f32[256,256]{1,0:T(8,128)S(1)}, u32[]{:S(2)}, u32[]{:S(2)}) %collective-permute-start.3) | collective-permute-done | bytes 262176 | tf_op jit(solution)/shard_map/ppermute | solution.py:18
  57.6 6.0 collective-permute-done.4
  63.8 6.7 collective-permute-done.5
  70.7 5.1 collective-permute-done.6
  75.9 2.0 collective-permute-start.7
  77.9 7.7 %collective-permute-done.7 = f32[256,256]{1,0:T(8,128)S(1)} collective-permute-done((f32[256,256]{1,0:T(8,128)S(1)}, f32[256,256]{1,0:T(8,128)S(1)}, u32[]{:S(2)}, u32[]{:S(2)}) %collective-permute-start.7) | collective-permute-done | bytes 262176 | tf_op jit(solution)/shard_map/ppermute | solution.py:18
  87.3 17.8 %while.26 = (s32[]{:T(128)}, f32[256,256]{0,1:T(8,128)S(1)}, f32[256,256]{1,0:T(8,128)S(1)}, s32[]{:T(128)}) while((s32[]{:T(128)}, f32[256,256]{0,1:T(8,128)S(1)}, f32[256,256]{1,0:T(8,128)S(1)}, s32[]{:T(128)}) %tuple.46), condition=%wide.region_2.0_spmd.clone, body=%wide.region_1.0_spmd.clone.sunk | while | flops 604241920 | bytes 3407925 | solution.py:32
  105.1 3.5 fusion.8
  108.6 2.7 convolution_bitcast_fusion.2
  111.4 254.4 %all-reduce.3.cloned.1.call-done = f32[512,256]{0,1:T(8,128)} async-done(((f32[512,256]{0,1:T(8,128)}), f32[512,256]{0,1:T(8,128)}) %all-reduce.3.cloned.1.call-update) | async-done | bytes 524304 | tf_op jit(solution)/shard_map/psum | solution.py:54
  365.8 2.9 fusion.17
  370.6 2.1 collective-permute-start.8
  374.0 7.5 %collective-permute-done.9 = f32[256,256]{1,0:T(8,128)S(1)} collective-permute-done((f32[256,256]{1,0:T(8,128)S(1)}, f32[256,256]{1,0:T(8,128)S(1)}, u32[]{:S(2)}, u32[]{:S(2)}) %collective-permute-start.9) | collective-permute-done | bytes 262176 | tf_op jit(solution)/shard_map/ppermute | solution.py:18
  381.5 3.1 collective-permute-start.10
  384.7 11.5 %collective-permute-done.10 = f32[256,256]{1,0:T(8,128)S(1)} collective-permute-done((f32[256,256]{1,0:T(8,128)S(1)}, f32[256,256]{1,0:T(8,128)S(1)}, u32[]{:S(2)}, u32[]{:S(2)}) %collective-permute-start.10) | collective-permute-done | bytes 262176 | tf_op jit(solution)/shard_map/ppermute | solution.py:18
  396.2 4.0 collective-permute-start.11
  400.3 12.9 %collective-permute-done.11 = f32[256,256]{1,0:T(8,128)S(1)} collective-permute-done((f32[256,256]{1,0:T(8,128)S(1)}, f32[256,256]{1,0:T(8,128)S(1)}, u32[]{:S(2)}, u32[]{:S(2)}) %collective-permute-start.11) | collective-permute-done | bytes 262176 | tf_op jit(solution)/shard_map/ppermute | solution.py:18
  414.1 5.6 collective-permute-done.12
  419.8 2.3 collective-permute-start.13
  422.1 4.7 collective-permute-done.13
  426.8 3.4 collective-permute-start.14
  430.3 4.2 collective-permute-done.14
  436.2 5.5 collective-permute-done.15
  443.2 17.8 %while.27 = (s32[]{:T(128)}, f32[256,256]{0,1:T(8,128)S(1)}, f32[256,256]{1,0:T(8,128)S(1)}, s32[]{:T(128)}) while((s32[]{:T(128)}, f32[256,256]{0,1:T(8,128)S(1)}, f32[256,256]{1,0:T(8,128)S(1)}, s32[]{:T(128)}) %tuple.49), condition=%wide.region_6.0_spmd.clone, body=%wide.region_5.0_spmd.clone.sunk | while | flops 604241920 | bytes 3407925 | solution.py:32
  460.9 6.4 broadcast_multiply_fusion
  467.3 2.7 fusion.19
  470.1 253.0 %all-reduce.5.cloned.1.call-done = f32[256,512]{1,0:T(8,128)} async-done(((f32[256,512]{1,0:T(8,128)}), f32[256,512]{1,0:T(8,128)}) %all-reduce.5.cloned.1.call-update) | async-done | bytes 524304 | tf_op jit(solution)/shard_map/psum | solution.py:60
  (165 shorter events, 50.6 us)
Async XLA Ops:
  7.2 1.6 copy-start
  7.2 358.6 %all-reduce.3.cloned.1.call-start = ((), (), s32[]{:S(2)}) async-start(), calls=%async_computation | async-start | bytes 1048576 | tf_op jit(solution)/shard_map/psum | solution.py:54
  10.4 3.7 copy-start.1
  14.1 4.5 collective-permute-start
  18.6 7.6 %collective-permute-start.1 = (f32[256,256]{1,0:T(8,128)S(1)}, f32[256,256]{1,0:T(8,128)S(1)}, u32[]{:S(2)}, u32[]{:S(2)}) collective-permute-start(f32[256,256]{1,0:T(8,128)S(1)} %add.58), channel_id=1, source_target_pairs={{0,8},{8,0},{4,12},{12,4},{16,24},{24,16},{20,28},{28,20},{32,40},... | collective-permute-start | bytes 786440 | tf_op jit(solution)/shard_map/ppermute | solution.py:18
  26.3 14.5 %collective-permute-start.2 = (f32[256,256]{1,0:T(8,128)S(1)}, f32[256,256]{1,0:T(8,128)S(1)}, u32[]{:S(2)}, u32[]{:S(2)}) collective-permute-start(f32[256,256]{1,0:T(8,128)S(1)} %add.59), channel_id=1, source_target_pairs={{0,16},{16,0},{4,20},{20,4},{8,24},{24,8},{12,28},{28,12},{32,48},... | collective-permute-start | bytes 786440 | tf_op jit(solution)/shard_map/ppermute | solution.py:18
  40.8 16.6 %collective-permute-start.3 = (f32[256,256]{1,0:T(8,128)S(1)}, f32[256,256]{1,0:T(8,128)S(1)}, u32[]{:S(2)}, u32[]{:S(2)}) collective-permute-start(f32[256,256]{1,0:T(8,128)S(1)} %add.60), channel_id=1, source_target_pairs={{0,32},{32,0},{4,36},{36,4},{8,40},{40,8},{12,44},{44,12},{16,48},... | collective-permute-start | bytes 786440 | tf_op jit(solution)/shard_map/ppermute | solution.py:18
  57.5 6.1 collective-permute-start.4
  63.7 6.8 collective-permute-start.5
  70.5 5.3 collective-permute-start.6
  75.9 9.8 %collective-permute-start.7 = (f32[256,256]{1,0:T(8,128)S(1)}, f32[256,256]{1,0:T(8,128)S(1)}, u32[]{:S(2)}, u32[]{:S(2)}) collective-permute-start(f32[256,256]{1,0:T(8,128)S(1)} %add.64), channel_id=1, source_target_pairs={{0,2},{2,0},{1,3},{3,1},{4,6},{6,4},{5,7},{7,5},{8,10},{10,8},{9,1... | collective-permute-start | bytes 786440 | tf_op jit(solution)/shard_map/ppermute | solution.py:18
  111.4 611.7 %all-reduce.5.cloned.1.call-start = ((), (), s32[]{:S(2)}) async-start(), calls=%async_computation.1 | async-start | bytes 1048576 | tf_op jit(solution)/shard_map/psum | solution.py:60
  368.7 1.9 copy-start.2
  370.6 3.3 collective-permute-start.8
  373.9 7.6 %collective-permute-start.9 = (f32[256,256]{1,0:T(8,128)S(1)}, f32[256,256]{1,0:T(8,128)S(1)}, u32[]{:S(2)}, u32[]{:S(2)}) collective-permute-start(f32[256,256]{1,0:T(8,128)S(1)} %add.66), channel_id=1, source_target_pairs={{0,8},{8,0},{4,12},{12,4},{16,24},{24,16},{20,28},{28,20},{32,40},... | collective-permute-start | bytes 786440 | tf_op jit(solution)/shard_map/ppermute | solution.py:18
  381.5 14.7 %collective-permute-start.10 = (f32[256,256]{1,0:T(8,128)S(1)}, f32[256,256]{1,0:T(8,128)S(1)}, u32[]{:S(2)}, u32[]{:S(2)}) collective-permute-start(f32[256,256]{1,0:T(8,128)S(1)} %add.67), channel_id=1, source_target_pairs={{0,16},{16,0},{4,20},{20,4},{8,24},{24,8},{12,28},{28,12},{32,48},... | collective-permute-start | bytes 786440 | tf_op jit(solution)/shard_map/ppermute | solution.py:18
  396.2 16.9 %collective-permute-start.11 = (f32[256,256]{1,0:T(8,128)S(1)}, f32[256,256]{1,0:T(8,128)S(1)}, u32[]{:S(2)}, u32[]{:S(2)}) collective-permute-start(f32[256,256]{1,0:T(8,128)S(1)} %add.68), channel_id=1, source_target_pairs={{0,32},{32,0},{4,36},{36,4},{8,40},{40,8},{12,44},{44,12},{16,48},... | collective-permute-start | bytes 786440 | tf_op jit(solution)/shard_map/ppermute | solution.py:18
  413.2 6.5 collective-permute-start.12
  419.8 7.0 collective-permute-start.13
  426.8 7.6 %collective-permute-start.14 = (f32[256,256]{1,0:T(8,128)S(1)}, f32[256,256]{1,0:T(8,128)S(1)}, u32[]{:S(2)}, u32[]{:S(2)}) collective-permute-start(f32[256,256]{1,0:T(8,128)S(1)} %add.71), channel_id=1, source_target_pairs={{0,1},{1,0},{2,3},{3,2},{4,5},{5,4},{6,7},{7,6},{8,9},{9,8},{10,11... | collective-permute-start | bytes 786440 | tf_op jit(solution)/shard_map/ppermute | solution.py:18
  434.5 7.1 collective-permute-start.15
Sparse Core Ops, SparseCore 0:
  111.5 254.2 all-reduce.2
  470.2 252.8 all-reduce.4
where the time goes:
time: 733 us; the launch traced here: 732 us
  waiting for transfers between devices  619 us (84%)
  matrix products  58.7 us (8%)
  starting transfers between devices  30.2 us (4%)
  between operations  15.8 us (2%)
    psum x1, waiting for transfers between devices, on_device(): power = lax.psum(local_power, ('rows', 'grp'))  254 us
    psum x1, waiting for transfers between devices, on_device(): coeff = lax.psum(local_coeff, ('rows', 'grp'))  253 us
    ppermute x16, waiting for transfers between devices, partner(): return lax.ppermute(block, axis, route)  112 us
    ppermute x16, starting transfers between devices, partner(): return lax.ppermute(block, axis, route)  30.2 us
  transfers between devices with their start and end apart: 18, of which 18 were waited for; matrix products, arithmetic and copies ran while one was open for 0% of the time, Pallas kernels for 0%

commit v1 on v0

v1 whole, which is shorter than its diff:
```python
import functools
import math

import jax
import jax.numpy as jnp
from jax import lax
from jax.experimental import pallas as pl
from jax.experimental.pallas import tpu as pltpu
from jax.sharding import Mesh, PartitionSpec as P

SWEEPS = 12
BLOCK = 256
F32 = jnp.float32
BF16 = jnp.bfloat16


def dot(a, b):
    return jnp.dot(a, b, preferred_element_type=F32)


def split2(x):
    high = x.astype(BF16)
    return high, (x - high.astype(F32)).astype(BF16)


def split3(x):
    high = x.astype(BF16)
    rest = x - high.astype(F32)
    mid = rest.astype(BF16)
    return high, mid, (rest - mid.astype(F32)).astype(BF16)


def times(a, b):
    if len(a) == 3 and len(b) == 3:
        low = dot(a[0], b[2]) + dot(a[1], b[1]) + dot(a[2], b[0])
        return low + (dot(a[0], b[1]) + dot(a[1], b[0])) + dot(a[0], b[0])
    total = None
    for part in reversed(a):
        for other in reversed(b):
            term = dot(part, other)
            total = term if total is None else total + term
    return total


def inverse_root(gram):
    n = gram.shape[0]
    scale = jnp.sqrt(jnp.sum(gram * gram))
    eye = lax.broadcasted_iota(jnp.int32, (n, n), 0) == lax.broadcasted_iota(jnp.int32, (n, n), 1)

    def advance(w, parts):
        square = times(parts, parts)
        return 2.25 * w - 1.5 * square + 0.25 * times(split2(square), parts)

    def sweep(index, carry):
        w, z = carry
        parts = split2(w)
        return advance(w, parts), 1.5 * z - 0.5 * times(split2(z), parts)

    w = gram * (1.0 / scale)
    z = jnp.where(eye, 1.5, 0.0) - 0.5 * w
    w = advance(w, split2(w))
    w, z = lax.fori_loop(0, SWEEPS - 2, sweep, (w, z))
    z = 1.5 * z - 0.5 * times(split2(z), split2(w))
    return z * (1.0 / jnp.sqrt(scale))


def finish(size, total_ref, sketch_ref, table_hbm, basis_hbm, coeff_ref, table, basis, in_sem, out_sem):
    fetch = pltpu.make_async_copy(table_hbm, table, in_sem)
    fetch.start()
    k = sketch_ref.shape[1]
    corner = total_ref[k : 2 * k, :]
    upper = jnp.concatenate([total_ref[0:k, :], corner], 1)
    lower = jnp.concatenate([corner.T, total_ref[2 * k : 3 * k, :]], 1)
    total = split3(jnp.concatenate([upper, lower], 0))
    sketch = sketch_ref[...]
    sketch_t = sketch.astype(F32).T.astype(BF16)
    first = split3(times(total, (sketch,)))
    first_inverse = inverse_root(times((sketch_t,), first))
    power = times(first, split3(first_inverse))
    power_parts = split3(power)
    table_power = split3(times(total, power_parts))
    second_inverse = split3(inverse_root(times(split3(power.T), table_power)))
    weight = split3(times(power_parts, second_inverse) * size)
    fetch.wait()
    copies = []
    for index in range(table.shape[0] // BLOCK):
        rows = pl.ds(index * BLOCK, BLOCK)
        basis[rows, :] = times((table[rows, :],), weight)
        copy = pltpu.make_async_copy(basis.at[rows], basis_hbm.at[rows], out_sem.at[index])
        copy.start()
        copies.append(copy)
    coeff_ref[...] = times(table_power, second_inverse).T * (1.0 / size)
    for copy in copies:
        copy.wait()


def finish_call(size, total, sketch, table):
    rows, n = table.shape
    k = sketch.shape[1]
    vmem = pl.BlockSpec(memory_space=pltpu.VMEM)
    hbm = pl.BlockSpec(memory_space=pl.ANY)
    return pl.pallas_call(
        functools.partial(finish, size),
        out_shape=(jax.ShapeDtypeStruct((rows, k), F32), jax.ShapeDtypeStruct((k, n), F32)),
        in_specs=[vmem, vmem, hbm],
        out_specs=(hbm, vmem),
        scratch_shapes=[
            pltpu.VMEM((rows, n), BF16),
            pltpu.VMEM((rows, k), F32),
            pltpu.SemaphoreType.DMA,
            pltpu.SemaphoreType.DMA((rows // BLOCK,)),
        ],
        compiler_params=pltpu.CompilerParams(vmem_limit_bytes=48 * 2**20),
    )(total, sketch, table)


def scatter_sum(block, axes):
    return jnp.sum(lax.all_to_all(block, axes, 0, 0), 0)


def gather(block, axes):
    count = lax.axis_size(axes)
    copies = jnp.broadcast_to(block[None], (count,) + block.shape)
    return lax.all_to_all(copies, axes, 0, 0)


def summed(local):
    plane = ("x", "y")
    core = lax.axis_index("core")
    swap = [(0, 1), (1, 0)]
    halves = local.reshape((2, -1) + local.shape[1:])
    keep = lax.dynamic_index_in_dim(halves, core, 0, False)
    send = lax.dynamic_index_in_dim(halves, 1 - core, 0, False)
    half = keep + lax.ppermute(send, "core", swap)
    part = scatter_sum(half.reshape((lax.axis_size(plane), -1) + half.shape[1:]), plane)
    part = jnp.sum(gather(part, "z"), 0)
    half = gather(part, plane).reshape(half.shape)
    other = lax.ppermute(half, "core", swap)
    first = jnp.where(core == 0, half, other)
    second = jnp.where(core == 0, other, half)
    return jnp.concatenate([first, second], 0)


def on_device(table, sketch):
    k = sketch.shape[1]
    count = table.shape[0] * lax.axis_size(("x", "z", "core", "y"))
    left, right = table[:, :k], table[:, k:]

    def gram(a, b):
        return jnp.einsum("rn,rm->nm", a, b, preferred_element_type=F32)

    local = jnp.concatenate([gram(left, left), gram(left, right), gram(right, right)], 0)
    return finish_call(math.sqrt(count), summed(local), sketch, table)


def solution(mesh):
    fine = Mesh(mesh.devices.reshape(4, 8, 2, 4), ("x", "z", "core", "y"))
    split = P(("x", "z", "core", "y"), None)
    return jax.shard_map(
        on_device, mesh=fine, in_specs=(split, P()), out_specs=(split, P()), check_vma=False
    )
```

time: 733 us -> 87.3 us (0.12)
  waiting for transfers between devices: 619 us -> 2.91 us
  matrix products: 58.7 us -> 5.41 us
  blocking collectives: 0 us -> 42.2 us
  Pallas kernels: 0 us -> 26.3 us
  starting transfers between devices: 30.2 us -> 7.45 us
  between operations: 15.8 us -> 0.72 us
    psum x2 -> x0, waiting for transfers between devices: 507 us -> none  [the longest x1 254 us: on_device(): power = lax.psum(local_power, ('rows', 'grp'))]
    ppermute x16 -> x2, waiting for transfers between devices: 112 us -> 2.91 us  [the longest x1 1.56 us: summed(): half = keep + lax.ppermute(send, 'core', swap)]
    dot_general x80 -> x3, matrix products: 58.7 us -> 5.41 us  [gram(): return jnp.einsum('rn,rm->nm', a, b, preferred_element_type=F32)]
    all_to_all x0 -> x3, blocking collectives: none -> 42.2 us  [the longest x2 28.1 us: gather(): return lax.all_to_all(copies, axes, 0, 0)]
    pallas_call x0 -> x1, Pallas kernels: none -> 26.3 us  [finish_call(): pl.pallas_call(functools.partial(finish, size), out_shape=(jax.ShapeDtype...]
    ppermute x16 -> x2, starting transfers between devices: 30.2 us -> 7.45 us  [the longest x1 4.2 us: summed(): other = lax.ppermute(half, 'core', swap)]
  transfers between devices with their start and end apart: 18 -> 2, of which waited for: 18 -> 2; matrix products, arithmetic and copies ran while one was open for 0% -> 0% of each run, Pallas kernels for 0% -> 0%
where the time goes in v1:
time: 87.3 us; the launch traced here: 87 us
  blocking collectives  42.2 us (48%)
  Pallas kernels  26.3 us (30%)
  starting transfers between devices  7.45 us (9%)
  matrix products  5.41 us (6%)
  waiting for transfers between devices  2.91 us (3%)
  other arithmetic  1.2 us (1%)
    all_to_all x2, blocking collectives, gather(): return lax.all_to_all(copies, axes, 0, 0)  28.1 us
    pallas_call x1, Pallas kernels, finish_call(): pl.pallas_call(functools.partial(finish, size), out_shape=(jax.ShapeDtype...  26.3 us
    all_to_all x1, blocking collectives, scatter_sum(): return jnp.sum(lax.all_to_all(block, axes, 0, 0), 0)  14.1 us
    dot_general x3, matrix products, gram(): return jnp.einsum('rn,rm->nm', a, b, preferred_element_type=F32)  5.41 us
    ppermute x1, starting transfers between devices, summed(): other = lax.ppermute(half, 'core', swap)  4.2 us
    ppermute x1, starting transfers between devices, summed(): half = keep + lax.ppermute(send, 'core', swap)  3.24 us
  transfers between devices with their start and end apart: 2, of which 2 were waited for; matrix products, arithmetic and copies ran while one was open for 0% of the time, Pallas kernels for 0%

profile of v1, /device:TPU:1, one launch (start us, length us, event | category | flops | bytes accessed | tf_op | source)
XLA Modules:
  0.0 87.0 jit_solution(2958509270614961683)
XLA Ops:
  0.6 0.0 copy-start
  0.6 2.2 %fusion = f32[256,256]{1,0:T(8,128)S(1)} fusion(bf16[2048,512]{1,0:T(8,128)(2,1)} %table_hbm.1), kind=kOutput, calls=%fused_computation | convolution fusion | flops 268435456 | bytes 1310720 | tf_op jit(solution)/shard_map/rn,rm->nm/dot_general | solution.py:150
  2.8 2.1 %fusion.5 = f32[256,256]{1,0:T(8,128)S(1)} fusion(bf16[2048,512]{1,0:T(8,128)(2,1)} %table_hbm.1), kind=kOutput, calls=%fused_computation.5 | convolution fusion | flops 268435456 | bytes 1310720 | tf_op jit(solution)/shard_map/rn,rm->nm/dot_general | solution.py:150
  4.9 0.0 copy-done
  4.9 1.2 %fusion.2 = f32[256,256]{1,0:T(8,128)} fusion(bf16[2048,512]{1,0:T(8,128)(2,1)S(1)} %copy-done), kind=kOutput, calls=%fused_computation.2 | convolution fusion | flops 268435456 | bytes 2359296 | tf_op jit(solution)/shard_map/rn,rm->nm/dot_general | solution.py:150
  6.1 1.0 %pad_maximum_fusion = f32[768,256]{1,0:T(8,128)S(1)} fusion(f32[256,256]{1,0:T(8,128)S(1)} %fusion, f32[256,256]{1,0:T(8,128)} %fusion.2, f32[256,256]{1,0:T(8,128)S(1)} %fusion.5), kind=kLoop, calls=%fused_computation.7 | loop fusion | flops 393216 | bytes 1572864 | tf_op jit(solution)/shard_map/concatenate | solution.py:152
  7.1 0.8 dynamic-slice_bitcast_fusion
  7.9 3.2 %collective-permute-start = (f32[384,256]{1,0:T(8,128)}, f32[384,256]{1,0:T(8,128)S(1)}, u32[]{:S(2)}, u32[]{:S(2)}) collective-permute-start(f32[384,256]{1,0:T(8,128)} %dynamic-slice_bitcast_fusion), channel_id=1, source_target_pairs={{0,4},{4,0},{1,5},{5,1},{2,6},{6,2},{3,7},{7,3},{8,12},{12,8},{9,1... | collective-permute-start | bytes 1179656 | tf_op jit(solution)/shard_map/ppermute | solution.py:134
  11.1 1.6 %collective-permute-done = f32[384,256]{1,0:T(8,128)S(1)} collective-permute-done((f32[384,256]{1,0:T(8,128)}, f32[384,256]{1,0:T(8,128)S(1)}, u32[]{:S(2)}, u32[]{:S(2)}) %collective-permute-start) | collective-permute-done | bytes 393248 | tf_op jit(solution)/shard_map/ppermute | solution.py:134
  12.7 0.1 bitcast_add_fusion
  12.7 14.1 %all_to_all.15 = f32[16,24,256]{2,1,0:T(8,128)S(1)} all-to-all(f32[16,24,256]{2,1,0:T(8,128)S(1)} %bitcast.12), channel_id=1, replica_groups=mesh['x'=4,'z'=8,'core'=2,'y'=4] {'x','y'}, dimensions={0} | all-to-all | bytes 786432 | tf_op jit(solution)/shard_map/all_to_all | solution.py:118
  26.8 16.7 %all_to_all.16 = f32[8,24,256]{2,1,0:T(8,128)S(1)} all-to-all(f32[8,24,256]{2,1,0:T(8,128)S(1)} %broadcast_in_dim.4), channel_id=1, replica_groups=mesh['x'=4,'z'=8,'core'=2,'y'=4] {'z'}, dimensions={0} | all-to-all | bytes 393216 | tf_op jit(solution)/shard_map/all_to_all | solution.py:124
  43.5 0.0 copy-start.1
  43.6 11.5 %all_to_all.17 = f32[16,24,256]{2,1,0:T(8,128)S(1)} all-to-all(f32[16,24,256]{2,1,0:T(8,128)S(1)} %broadcast_in_dim.5), channel_id=1, replica_groups=mesh['x'=4,'z'=8,'core'=2,'y'=4] {'x','y'}, dimensions={0} | all-to-all | bytes 786432 | tf_op jit(solution)/shard_map/all_to_all | solution.py:124
  55.0 4.2 %collective-permute-start.1 = (f32[384,256]{1,0:T(8,128)S(1)}, f32[384,256]{1,0:T(8,128)S(1)}, u32[]{:S(2)}, u32[]{:S(2)}) collective-permute-start(f32[384,256]{1,0:T(8,128)S(1)} %bitcast.11), channel_id=1, source_target_pairs={{0,4},{4,0},{1,5},{5,1},{2,6},{6,2},{3,7},{7,3},{8,12},{12,8},{9,1... | collective-permute-start | bytes 1179656 | tf_op jit(solution)/shard_map/ppermute | solution.py:138
  59.2 1.3 %collective-permute-done.1 = f32[384,256]{1,0:T(8,128)S(1)} collective-permute-done((f32[384,256]{1,0:T(8,128)S(1)}, f32[384,256]{1,0:T(8,128)S(1)}, u32[]{:S(2)}, u32[]{:S(2)}) %collective-permute-start.1) | collective-permute-done | bytes 393248 | tf_op jit(solution)/shard_map/ppermute | solution.py:138
  60.6 0.1 broadcast_select_fusion.1
  60.7 0.1 pad_maximum_fusion.1.total_ref
  60.7 0.0 copy-done.1
  60.7 26.3 %shard_map.41 = (f32[2048,256]{1,0:T(8,128)}, f32[256,512]{1,0:T(8,128)}) custom-call(f32[768,256]{1,0:T(8,128)S(1)} %pad_maximum_fusion.1.total_ref, bf16[512,256]{1,0:T(8,128)(2,1)S(1)} %copy-done.1, bf16[2048,512]{1,0:T(8,128)(2,1)S(1)} %copy-done), custom_call_target="tpu_custom_call" | custom-call | tf_op jit(solution)/shard_map/pallas_call | solution.py:102
  (4 shorter events, 0.1 us)
Async XLA Ops:
  0.6 4.3 %copy-start = (bf16[2048,512]{1,0:T(8,128)(2,1)S(1)}, bf16[2048,512]{1,0:T(8,128)(2,1)}, u32[]{:S(2)}) copy-start(bf16[2048,512]{1,0:T(8,128)(2,1)} %table_hbm.1) | copy-start | bytes 6291460
  7.9 4.8 %collective-permute-start = (f32[384,256]{1,0:T(8,128)}, f32[384,256]{1,0:T(8,128)S(1)}, u32[]{:S(2)}, u32[]{:S(2)}) collective-permute-start(f32[384,256]{1,0:T(8,128)} %dynamic-slice_bitcast_fusion), channel_id=1, source_target_pairs={{0,4},{4,0},{1,5},{5,1},{2,6},{6,2},{3,7},{7,3},{8,12},{12,8},{9,1... | collective-permute-start | bytes 1179656 | tf_op jit(solution)/shard_map/ppermute | solution.py:134
  43.5 17.2 %copy-start.1 = (bf16[512,256]{1,0:T(8,128)(2,1)S(1)}, bf16[512,256]{1,0:T(8,128)(2,1)}, u32[]{:S(2)}) copy-start(bf16[512,256]{1,0:T(8,128)(2,1)} %sketch_ref.1) | copy-start | bytes 786436
  55.0 5.6 %collective-permute-start.1 = (f32[384,256]{1,0:T(8,128)S(1)}, f32[384,256]{1,0:T(8,128)S(1)}, u32[]{:S(2)}, u32[]{:S(2)}) collective-permute-start(f32[384,256]{1,0:T(8,128)S(1)} %bitcast.11), channel_id=1, source_target_pairs={{0,4},{4,0},{1,5},{5,1},{2,6},{6,2},{3,7},{7,3},{8,12},{12,8},{9,1... | collective-permute-start | bytes 1179656 | tf_op jit(solution)/shard_map/ppermute | solution.py:138

commit v2 on v1

v2 whole, which is shorter than its diff:
```python
import functools
import math

import jax
import jax.numpy as jnp
from jax import lax
from jax.experimental import pallas as pl
from jax.experimental.pallas import tpu as pltpu
from jax.sharding import Mesh, PartitionSpec as P

SWEEPS = 12
NEAR = 8
BLOCK = 256
TILE = 128
PAIRS = [(i, j) for i in range(4) for j in range(i, 4)]
HALF = len(PAIRS) // 2 * TILE
F32 = jnp.float32
BF16 = jnp.bfloat16
VMEM = pl.BlockSpec(memory_space=pltpu.VMEM)
HBM = pl.BlockSpec(memory_space=pl.ANY)
PARAMS = pltpu.CompilerParams(vmem_limit_bytes=48 * 2**20)


def dot(a, b):
    return jnp.dot(a, b, preferred_element_type=F32)


def split(x):
    high = x.astype(BF16)
    return high, (x - high.astype(F32)).astype(BF16)


def times(a, b):
    total = None
    for part in reversed(a):
        for other in reversed(b):
            term = dot(part, other)
            total = term if total is None else total + term
    return total


def product(a, b, low):
    half = a[0].shape[0] // 2
    out = []
    for start in (0, half):
        high = a[0][start : start + half]
        rest = a[1][start : start + half]
        both = jnp.concatenate([high, rest], 0)
        large = dot(both, b[0])
        small = dot(both if low else high, b[1])
        sums = small[:half] + large[half:]
        if low:
            sums = small[half:] + sums
        out.append(sums + large[:half])
    return jnp.concatenate(out, 0)


def inverse_root(gram):
    n = gram.shape[0]
    scale = jnp.sqrt(jnp.sum(gram * gram))
    eye = lax.broadcasted_iota(jnp.int32, (n, n), 0) == lax.broadcasted_iota(jnp.int32, (n, n), 1)

    def far(index, carry):
        w, z = carry
        parts = split(w)
        square = product(parts, parts, True)
        z = 1.5 * z - 0.5 * product(split(z), parts, False)
        cube = product(split(square), parts, False)
        return 2.25 * w - 1.5 * square + 0.25 * cube, z

    def near(index, carry):
        e, z = carry
        parts = split(e)
        square = product(parts, parts, False)
        z = z + product(split(z), parts, False)
        return 1.5 * square + product(split(square), parts, False), z

    w = gram * (1.0 / scale)
    z = jnp.where(eye, 1.5, 0.0) - 0.5 * w
    parts = split(w)
    square = product(parts, parts, True)
    w = 2.25 * w - 1.5 * square + 0.25 * product(split(square), parts, False)
    w, z = lax.fori_loop(1, NEAR, far, (w, z))
    e = jnp.where(eye, 0.5, 0.0) - 0.5 * w
    e, z = lax.fori_loop(NEAR, SWEEPS - 1, near, (e, z))
    z = z + product(split(z), split(e), False)
    return z * (1.0 / jnp.sqrt(scale))


def gram_kernel(table_ref, keep_ref, send_ref):
    table = table_ref[...]
    k = table.shape[1] // 2

    def gram(a, b):
        return lax.dot_general(a, b, (((0,), (0,)), ((), ())), preferred_element_type=F32)

    upper = gram(table[:, :k], table)
    lower = gram(table[:, k:], table[:, k:])
    tiles = []
    for i, j in PAIRS:
        source, row, col = (upper, i, j) if i < 2 else (lower, i - 2, j - 2)
        tiles.append(source[row * TILE : (row + 1) * TILE, col * TILE : (col + 1) * TILE])
    count = len(PAIRS) // 2
    core = lax.axis_index("core")

    def store(mine, others):
        for n in range(count):
            rows = pl.ds(n * TILE, TILE)
            keep_ref[rows, :] = mine[n]
            send_ref[rows, :] = others[n]

    @pl.when(core == 0)
    def _():
        store(tiles[:count], tiles[count:])

    @pl.when(core != 0)
    def _():
        store(tiles[count:], tiles[:count])


def gram_call(table):
    half = jax.ShapeDtypeStruct((HALF, TILE), F32)
    return pl.pallas_call(
        gram_kernel,
        out_shape=(half, half),
        in_specs=[VMEM],
        out_specs=(VMEM, VMEM),
        compiler_params=PARAMS,
    )(table)


def finish(size, mine_ref, other_ref, sketch_ref, table_hbm, basis_hbm, coeff_hbm, table, basis, coeff, in_sem, out_sem):
    fetch = pltpu.make_async_copy(table_hbm, table, in_sem)
    fetch.start()
    first_core = lax.axis_index("core") == 0
    mine, other = mine_ref[...], other_ref[...]
    tiles = {}
    for n, half in enumerate((jnp.where(first_core, mine, other), jnp.where(first_core, other, mine))):
        for m in range(HALF // TILE):
            i, j = PAIRS[n * (HALF // TILE) + m]
            tile = half[m * TILE : (m + 1) * TILE, :]
            tiles[i, j] = tile
            if i != j:
                tiles[j, i] = tile.T
    total = split(jnp.concatenate([jnp.concatenate([tiles[i, j] for j in range(4)], 1) for i in range(4)], 0))
    sketch = sketch_ref[...]
    first = split(times(total, (sketch,)))
    power = times(first, split(inverse_root(times((sketch.astype(F32).T.astype(BF16),), first))))
    parts = split(power)
    table_power = split(times(total, parts))
    second_inverse = split(inverse_root(times(split(power.T), table_power)))
    weight = split(times(parts, second_inverse) * size)
    fetch.wait()
    copies = []
    blocks = table.shape[0] // BLOCK
    for index in range(blocks):
        rows = pl.ds(index * BLOCK, BLOCK)
        basis[rows, :] = times((table[rows, :],), weight)
        copy = pltpu.make_async_copy(basis.at[rows], basis_hbm.at[rows], out_sem.at[index])
        copy.start()
        copies.append(copy)
        if index == blocks // 2:
            coeff[...] = times(table_power, second_inverse).T * (1.0 / size)
            copy = pltpu.make_async_copy(coeff, coeff_hbm, out_sem.at[blocks])
            copy.start()
            copies.append(copy)
    for copy in copies:
        copy.wait()


def finish_call(size, mine, other, sketch, table):
    rows, n = table.shape
    k = sketch.shape[1]
    return pl.pallas_call(
        functools.partial(finish, size),
        out_shape=(jax.ShapeDtypeStruct((rows, k), F32), jax.ShapeDtypeStruct((k, n), F32)),
        in_specs=[VMEM, VMEM, VMEM, HBM],
        out_specs=(HBM, HBM),
        scratch_shapes=[
            pltpu.VMEM((rows, n), BF16),
            pltpu.VMEM((rows, k), F32),
            pltpu.VMEM((k, n), F32),
            pltpu.SemaphoreType.DMA,
            pltpu.SemaphoreType.DMA((rows // BLOCK + 1,)),
        ],
        compiler_params=PARAMS,
    )(mine, other, sketch, table)


def scatter_sum(block, axes):
    return jnp.sum(lax.all_to_all(block, axes, 0, 0), 0)


def gather(block, axes):
    count = lax.axis_size(axes)
    copies = jnp.broadcast_to(block[None], (count,) + block.shape)
    return lax.all_to_all(copies, axes, 0, 0)


def on_device(table, sketch):
    count = table.shape[0] * lax.axis_size(("x", "z", "core", "y"))
    plane = ("x", "y")
    swap = [(0, 1), (1, 0)]
    keep, send = gram_call(table)
    half = keep + lax.ppermute(send, "core", swap)
    part = scatter_sum(half.reshape(lax.axis_size(plane), -1, TILE), plane)
    part = jnp.sum(gather(part, "z"), 0)
    mine = gather(part, plane).reshape(HALF, TILE)
    other = lax.ppermute(mine, "core", swap)
    return finish_call(math.sqrt(count), mine, other, sketch, table)


def solution(mesh):
    fine = Mesh(mesh.devices.reshape(4, 8, 2, 4), ("x", "z", "core", "y"))
    split_rows = P(("x", "z", "core", "y"), None)
    return jax.shard_map(
        on_device, mesh=fine, in_specs=(split_rows, P()), out_specs=(split_rows, P()), check_vma=False
    )
```

time: 87.3 us -> 74.9 us (0.86)
  matrix products: 5.41 us -> 0 us
  Pallas kernels: 26.3 us -> 21.5 us
  blocking collectives: 42.2 us -> 40.6 us
  other arithmetic: 1.2 us -> 0.07 us
    pallas_call x1, Pallas kernels: 26.3 us -> 20.5 us  [finish_call(): pl.pallas_call(functools.partial(finish, size), out_shape=(jax.ShapeDtype...]
    dot_general x3 -> x0, matrix products: 5.41 us -> none  [gram(): return jnp.einsum('rn,rm->nm', a, b, preferred_element_type=F32)]
    unnamed x4 -> x6, local copies, waits for them, and re-layouts: 0.01 us -> 1.6 us
    all_to_all x1, blocking collectives: 14.1 us -> 12.8 us  [scatter_sum(): return jnp.sum(lax.all_to_all(block, axes, 0, 0), 0)]
    pallas_call x0 -> x1, Pallas kernels: none -> 1.06 us  [gram_call(): pl.pallas_call(gram_kernel, out_shape=(half, half), in_specs=[VMEM], out_...]
    concatenate x2 -> x0, other arithmetic: 1.05 us -> none  [the longest x1 1 us: on_device(): jnp.concatenate([gram(left, left), gram(left, right), gram(right, right)]...]
where the time goes in v2:
time: 74.9 us; the launch traced here: 74.7 us
  blocking collectives  40.6 us (54%)
  Pallas kernels  21.5 us (29%)
  starting transfers between devices  7.63 us (10%)
  waiting for transfers between devices  2.51 us (3%)
  local copies, waits for them, and re-layouts  1.64 us (2%)
    all_to_all x2, blocking collectives, gather(): return lax.all_to_all(copies, axes, 0, 0)  27.9 us
    pallas_call x1, Pallas kernels, finish_call(): pl.pallas_call(functools.partial(finish, size), out_shape=(jax.ShapeDtype...  20.5 us
    all_to_all x1, blocking collectives, scatter_sum(): return jnp.sum(lax.all_to_all(block, axes, 0, 0), 0)  12.8 us
    ppermute x1, starting transfers between devices, on_device(): other = lax.ppermute(mine, 'core', swap)  4.32 us
    ppermute x1, starting transfers between devices, on_device(): half = keep + lax.ppermute(send, 'core', swap)  3.32 us
    unnamed x6, local copies, waits for them, and re-layouts  1.6 us
  transfers between devices with their start and end apart: 2, of which 2 were waited for; matrix products, arithmetic and copies ran while one was open for 0% of the time, Pallas kernels for 0%

profile of v2, /device:TPU:1, one launch (start us, length us, event | category | flops | bytes accessed | tf_op | source)
XLA Modules:
  0.0 74.7 jit_solution(3438390792605535358)
XLA Ops:
  0.6 0.0 copy-start
  0.6 1.6 %copy-done = bf16[2048,512]{1,0:T(8,128)(2,1)S(1)} copy-done((bf16[2048,512]{1,0:T(8,128)(2,1)S(1)}, bf16[2048,512]{1,0:T(8,128)(2,1)}, u32[]{:S(2)}) %copy-start) | copy-done | bytes 2097176
  2.2 1.1 %shard_map.41 = (f32[640,128]{1,0:T(8,128)S(1)}, f32[640,128]{1,0:T(8,128)S(1)}) custom-call(bf16[2048,512]{1,0:T(8,128)(2,1)S(1)} %copy-done), custom_call_target="tpu_custom_call" | custom-call | tf_op jit(solution)/shard_map/pallas_call | solution.py:123
  3.3 0.0 copy-start.1
  3.3 0.0 copy-start.2
  3.3 3.3 %collective-permute-start = (f32[640,128]{1,0:T(8,128)S(1)}, f32[640,128]{1,0:T(8,128)S(1)}, u32[]{:S(2)}, u32[]{:S(2)}) collective-permute-start(f32[640,128]{1,0:T(8,128)S(1)} %get-tuple-element.5), channel_id=1, source_target_pairs={{0,4},{4,0},{1,5},{5,1},{2,6},{6,2},{3,7},{7,3},{8,12},{12,8},{9,1... | collective-permute-start | bytes 983048 | tf_op jit(solution)/shard_map/ppermute | solution.py:205
  6.6 1.3 %collective-permute-done = f32[640,128]{1,0:T(8,128)S(1)} collective-permute-done((f32[640,128]{1,0:T(8,128)S(1)}, f32[640,128]{1,0:T(8,128)S(1)}, u32[]{:S(2)}, u32[]{:S(2)}) %collective-permute-start) | collective-permute-done | bytes 327712 | tf_op jit(solution)/shard_map/ppermute | solution.py:205
  7.9 12.8 %all_to_all.15 = f32[16,40,128]{2,1,0:T(8,128)S(1)} all-to-all(f32[16,40,128]{2,1,0:T(8,128)S(1)} %bitcast.4), channel_id=1, replica_groups=mesh['x'=4,'z'=8,'core'=2,'y'=4] {'x','y'}, dimensions={0} | all-to-all | bytes 655360 | tf_op jit(solution)/shard_map/all_to_all | solution.py:191
  20.7 16.4 %all_to_all.16 = f32[8,40,128]{2,1,0:T(8,128)S(1)} all-to-all(f32[8,40,128]{2,1,0:T(8,128)S(1)} %broadcast_in_dim.4), channel_id=1, replica_groups=mesh['x'=4,'z'=8,'core'=2,'y'=4] {'z'}, dimensions={0} | all-to-all | bytes 327680 | tf_op jit(solution)/shard_map/all_to_all | solution.py:197
  37.1 11.5 %all_to_all.17 = f32[16,40,128]{2,1,0:T(8,128)S(1)} all-to-all(f32[16,40,128]{2,1,0:T(8,128)S(1)} %broadcast_in_dim.5), channel_id=1, replica_groups=mesh['x'=4,'z'=8,'core'=2,'y'=4] {'x','y'}, dimensions={0} | all-to-all | bytes 655360 | tf_op jit(solution)/shard_map/all_to_all | solution.py:197
  48.6 4.3 %collective-permute-start.1 = (f32[640,128]{1,0:T(8,128)S(1)}, f32[640,128]{1,0:T(8,128)S(1)}, u32[]{:S(2)}, u32[]{:S(2)}) collective-permute-start(f32[640,128]{1,0:T(8,128)S(1)} %bitcast.2), channel_id=1, source_target_pairs={{0,4},{4,0},{1,5},{5,1},{2,6},{6,2},{3,7},{7,3},{8,12},{12,8},{9,1... | collective-permute-start | bytes 983048 | tf_op jit(solution)/shard_map/ppermute | solution.py:209
  52.9 1.3 %collective-permute-done.1.other_ref = f32[640,128]{1,0:T(8,128)S(1)} collective-permute-done((f32[640,128]{1,0:T(8,128)S(1)}, f32[640,128]{1,0:T(8,128)S(1)}, u32[]{:S(2)}, u32[]{:S(2)}) %collective-permute-start.1) | collective-permute-done | bytes 327712 | tf_op jit(solution)/shard_map/ppermute | solution.py:209
  54.2 0.0 copy-done.1
  54.2 0.0 copy-done.2
  54.2 20.5 %shard_map.42 = (f32[2048,256]{1,0:T(8,128)}, f32[256,512]{1,0:T(8,128)}) custom-call(f32[640,128]{1,0:T(8,128)S(1)} %bitcast.3, f32[640,128]{1,0:T(8,128)S(1)} %collective-permute-done.1.other_ref, bf16[512,256]{1,0:T(8,128)(2,1)S(1)} %copy-done.2, bf16[2048,512]{1,0:T(8,128)(2,1)S(1)} %copy-done.1), custom_call_target="tpu_custom_call" | custom-call | tf_op jit(solution)/shard_map/pallas_call | solution.py:174
  (5 shorter events, 0.1 us)
Async XLA Ops:
  0.6 1.6 %copy-start = (bf16[2048,512]{1,0:T(8,128)(2,1)S(1)}, bf16[2048,512]{1,0:T(8,128)(2,1)}, u32[]{:S(2)}) copy-start(bf16[2048,512]{1,0:T(8,128)(2,1)} %table_hbm.1) | copy-start | bytes 6291460
  3.3 50.9 %copy-start.1 = (bf16[2048,512]{1,0:T(8,128)(2,1)S(1)}, bf16[2048,512]{1,0:T(8,128)(2,1)}, u32[]{:S(2)}) copy-start(bf16[2048,512]{1,0:T(8,128)(2,1)} %table_hbm.1) | copy-start | bytes 6291460
  3.3 50.9 %copy-start.2 = (bf16[512,256]{1,0:T(8,128)(2,1)S(1)}, bf16[512,256]{1,0:T(8,128)(2,1)}, u32[]{:S(2)}) copy-start(bf16[512,256]{1,0:T(8,128)(2,1)} %sketch_ref.1) | copy-start | bytes 786436
  3.3 4.6 %collective-permute-start = (f32[640,128]{1,0:T(8,128)S(1)}, f32[640,128]{1,0:T(8,128)S(1)}, u32[]{:S(2)}, u32[]{:S(2)}) collective-permute-start(f32[640,128]{1,0:T(8,128)S(1)} %get-tuple-element.5), channel_id=1, source_target_pairs={{0,4},{4,0},{1,5},{5,1},{2,6},{6,2},{3,7},{7,3},{8,12},{12,8},{9,1... | collective-permute-start | bytes 983048 | tf_op jit(solution)/shard_map/ppermute | solution.py:205
  48.6 5.6 %collective-permute-start.1 = (f32[640,128]{1,0:T(8,128)S(1)}, f32[640,128]{1,0:T(8,128)S(1)}, u32[]{:S(2)}, u32[]{:S(2)}) collective-permute-start(f32[640,128]{1,0:T(8,128)S(1)} %bitcast.2), channel_id=1, source_target_pairs={{0,4},{4,0},{1,5},{5,1},{2,6},{6,2},{3,7},{7,3},{8,12},{12,8},{9,1... | collective-permute-start | bytes 983048 | tf_op jit(solution)/shard_map/ppermute | solution.py:209

commit v3 on v2

--- a/solution.py
+++ b/solution.py
@@ -11,6 +11,7 @@
 SWEEPS = 12
 NEAR = 8
 BLOCK = 256
+STRIP = 128
 TILE = 128
 PAIRS = [(i, j) for i in range(4) for j in range(i, 4)]
 HALF = len(PAIRS) // 2 * TILE
@@ -30,59 +31,48 @@
     return high, (x - high.astype(F32)).astype(BF16)
 
 
-def times(a, b):
-    total = None
-    for part in reversed(a):
-        for other in reversed(b):
-            term = dot(part, other)
-            total = term if total is None else total + term
-    return total
-
-
-def product(a, b, low):
-    half = a[0].shape[0] // 2
+def product(a, b, low, strip=STRIP):
     out = []
-    for start in (0, half):
-        high = a[0][start : start + half]
-        rest = a[1][start : start + half]
-        both = jnp.concatenate([high, rest], 0)
+    for start in range(0, a[0].shape[0], strip):
+        rows = [part[start : start + strip] for part in a]
+        both = jnp.concatenate(rows, 0)
         large = dot(both, b[0])
-        small = dot(both if low else high, b[1])
-        sums = small[:half] + large[half:]
-        if low:
-            sums = small[half:] + sums
-        out.append(sums + large[:half])
+        sums = large[:strip]
+        if len(a) == 2:
+            sums = large[strip:] + sums if len(b) == 1 else sums
+        if len(b) == 2:
+            small = dot(both if low else rows[0], b[1])
+            rest = small[:strip]
+            if len(a) == 2:
+                rest = rest + large[strip:]
+                rest = small[strip:] + rest if low else rest
+            sums = rest + sums
+        out.append(sums)
     return jnp.concatenate(out, 0)
 
 
 def inverse_root(gram):
     n = gram.shape[0]
+    eye = lax.broadcasted_iota(jnp.int32, (n, n), 0) == lax.broadcasted_iota(jnp.int32, (n, n), 1)
+    parts = split(gram)
+    square = product(parts, parts, True)
     scale = jnp.sqrt(jnp.sum(gram * gram))
-    eye = lax.broadcasted_iota(jnp.int32, (n, n), 0) == lax.broadcasted_iota(jnp.int32, (n, n), 1)
-
-    def far(index, carry):
-        w, z = carry
-        parts = split(w)
+    factor = 0.5 / scale
+    x = gram * factor
+    square = (square * factor) * factor
+    z = jnp.where(eye, 1.5, 0.0) - x
+    x = 2.25 * x - 3.0 * square + product(split(square), split(x), False)
+    for _ in range(1, NEAR):
+        parts = split(x)
         square = product(parts, parts, True)
-        z = 1.5 * z - 0.5 * product(split(z), parts, False)
-        cube = product(split(square), parts, False)
-        return 2.25 * w - 1.5 * square + 0.25 * cube, z
-
-    def near(index, carry):
-        e, z = carry
+        z = 1.5 * z - product(split(z), parts, False)
+        x = 2.25 * x - 3.0 * square + product(split(square), parts, False)
+    e = jnp.where(eye, 0.5, 0.0) - x
+    for _ in range(NEAR, SWEEPS - 1):
         parts = split(e)
         square = product(parts, parts, False)
         z = z + product(split(z), parts, False)
-        return 1.5 * square + product(split(square), parts, False), z
-
-    w = gram * (1.0 / scale)
-    z = jnp.where(eye, 1.5, 0.0) - 0.5 * w
-    parts = split(w)
-    square = product(parts, parts, True)
-    w = 2.25 * w - 1.5 * square + 0.25 * product(split(square), parts, False)
-    w, z = lax.fori_loop(1, NEAR, far, (w, z))
-    e = jnp.where(eye, 0.5, 0.0) - 0.5 * w
-    e, z = lax.fori_loop(NEAR, SWEEPS - 1, near, (e, z))
+        e = 1.5 * square + product(split(square), parts, False)
     z = z + product(split(z), split(e), False)
     return z * (1.0 / jnp.sqrt(scale))
 
@@ -144,23 +134,24 @@
                 tiles[j, i] = tile.T
     total = split(jnp.concatenate([jnp.concatenate([tiles[i, j] for j in range(4)], 1) for i in range(4)], 0))
     sketch = sketch_ref[...]
-    first = split(times(total, (sketch,)))
-    power = times(first, split(inverse_root(times((sketch.astype(F32).T.astype(BF16),), first))))
+    first = split(product(total, (sketch,), True))
+    sketch_t = sketch.astype(F32).T.astype(BF16)
+    power = product(first, split(inverse_root(product((sketch_t,), first, True))), True)
     parts = split(power)
-    table_power = split(times(total, parts))
-    second_inverse = split(inverse_root(times(split(power.T), table_power)))
-    weight = split(times(parts, second_inverse) * size)
+    table_power = split(product(total, parts, True))
+    second_inverse = split(inverse_root(product(split(power.T), table_power, True)))
+    weight = split(product(parts, second_inverse, True) * size)
     fetch.wait()
     copies = []
     blocks = table.shape[0] // BLOCK
     for index in range(blocks):
         rows = pl.ds(index * BLOCK, BLOCK)
-        basis[rows, :] = times((table[rows, :],), weight)
+        basis[rows, :] = product((table[rows, :],), weight, True, BLOCK)
         copy = pltpu.make_async_copy(basis.at[rows], basis_hbm.at[rows], out_sem.at[index])
         copy.start()
         copies.append(copy)
-        if index == blocks // 2:
-            coeff[...] = times(table_power, second_inverse).T * (1.0 / size)
+        if index == 0:
+            coeff[...] = product(table_power, second_inverse, True).T * (1.0 / size)
             copy = pltpu.make_async_copy(coeff, coeff_hbm, out_sem.at[blocks])
             copy.start()
             copies.append(copy)

time: 74.9 us -> 71.3 us (0.952)
  Pallas kernels: 21.5 us -> 17.7 us
    pallas_call x1, Pallas kernels: 20.5 us -> 16.7 us  [finish_call(): pl.pallas_call(functools.partial(finish, size), out_shape=(jax.ShapeDtype...]
where the time goes in v3:
time: 71.3 us; the launch traced here: 71 us
  blocking collectives  40.6 us (57%)
  Pallas kernels  17.7 us (25%)
  starting transfers between devices  7.63 us (11%)
  waiting for transfers between devices  2.51 us (4%)
  local copies, waits for them, and re-layouts  1.64 us (2%)
  between operations  0.85 us (1%)
    all_to_all x2, blocking collectives, gather(): return lax.all_to_all(copies, axes, 0, 0)  27.9 us
    pallas_call x1, Pallas kernels, finish_call(): pl.pallas_call(functools.partial(finish, size), out_shape=(jax.ShapeDtype...  16.7 us
    all_to_all x1, blocking collectives, scatter_sum(): return jnp.sum(lax.all_to_all(block, axes, 0, 0), 0)  12.8 us
    ppermute x1, starting transfers between devices, on_device(): other = lax.ppermute(mine, 'core', swap)  4.32 us
    ppermute x1, starting transfers between devices, on_device(): half = keep + lax.ppermute(send, 'core', swap)  3.32 us
    unnamed x6, local copies, waits for them, and re-layouts  1.6 us
  transfers between devices with their start and end apart: 2, of which 2 were waited for; matrix products, arithmetic and copies ran while one was open for 0% of the time, Pallas kernels for 0%

profile of v3, /device:TPU:1, one launch (start us, length us, event | category | flops | bytes accessed | tf_op | source)
XLA Modules:
  0.0 71.0 jit_solution(10955318539318885420)
XLA Ops:
  0.6 0.0 copy-start
  0.6 1.6 %copy-done = bf16[2048,512]{1,0:T(8,128)(2,1)S(1)} copy-done((bf16[2048,512]{1,0:T(8,128)(2,1)S(1)}, bf16[2048,512]{1,0:T(8,128)(2,1)}, u32[]{:S(2)}) %copy-start) | copy-done | bytes 2097176
  2.2 1.1 %shard_map.41 = (f32[640,128]{1,0:T(8,128)S(1)}, f32[640,128]{1,0:T(8,128)S(1)}) custom-call(bf16[2048,512]{1,0:T(8,128)(2,1)S(1)} %copy-done), custom_call_target="tpu_custom_call" | custom-call | tf_op jit(solution)/shard_map/pallas_call | solution.py:113
  3.3 0.0 copy-start.1
  3.3 0.0 copy-start.2
  3.3 3.3 %collective-permute-start = (f32[640,128]{1,0:T(8,128)S(1)}, f32[640,128]{1,0:T(8,128)S(1)}, u32[]{:S(2)}, u32[]{:S(2)}) collective-permute-start(f32[640,128]{1,0:T(8,128)S(1)} %get-tuple-element.5), channel_id=1, source_target_pairs={{0,4},{4,0},{1,5},{5,1},{2,6},{6,2},{3,7},{7,3},{8,12},{12,8},{9,1... | collective-permute-start | bytes 983048 | tf_op jit(solution)/shard_map/ppermute | solution.py:196
  6.6 1.3 %collective-permute-done = f32[640,128]{1,0:T(8,128)S(1)} collective-permute-done((f32[640,128]{1,0:T(8,128)S(1)}, f32[640,128]{1,0:T(8,128)S(1)}, u32[]{:S(2)}, u32[]{:S(2)}) %collective-permute-start) | collective-permute-done | bytes 327712 | tf_op jit(solution)/shard_map/ppermute | solution.py:196
  7.9 12.8 %all_to_all.15 = f32[16,40,128]{2,1,0:T(8,128)S(1)} all-to-all(f32[16,40,128]{2,1,0:T(8,128)S(1)} %bitcast.4), channel_id=1, replica_groups=mesh['x'=4,'z'=8,'core'=2,'y'=4] {'x','y'}, dimensions={0} | all-to-all | bytes 655360 | tf_op jit(solution)/shard_map/all_to_all | solution.py:182
  20.7 16.4 %all_to_all.16 = f32[8,40,128]{2,1,0:T(8,128)S(1)} all-to-all(f32[8,40,128]{2,1,0:T(8,128)S(1)} %broadcast_in_dim.4), channel_id=1, replica_groups=mesh['x'=4,'z'=8,'core'=2,'y'=4] {'z'}, dimensions={0} | all-to-all | bytes 327680 | tf_op jit(solution)/shard_map/all_to_all | solution.py:188
  37.1 11.5 %all_to_all.17 = f32[16,40,128]{2,1,0:T(8,128)S(1)} all-to-all(f32[16,40,128]{2,1,0:T(8,128)S(1)} %broadcast_in_dim.5), channel_id=1, replica_groups=mesh['x'=4,'z'=8,'core'=2,'y'=4] {'x','y'}, dimensions={0} | all-to-all | bytes 655360 | tf_op jit(solution)/shard_map/all_to_all | solution.py:188
  48.6 4.3 %collective-permute-start.1 = (f32[640,128]{1,0:T(8,128)S(1)}, f32[640,128]{1,0:T(8,128)S(1)}, u32[]{:S(2)}, u32[]{:S(2)}) collective-permute-start(f32[640,128]{1,0:T(8,128)S(1)} %bitcast.2), channel_id=1, source_target_pairs={{0,4},{4,0},{1,5},{5,1},{2,6},{6,2},{3,7},{7,3},{8,12},{12,8},{9,1... | collective-permute-start | bytes 983048 | tf_op jit(solution)/shard_map/ppermute | solution.py:200
  52.9 1.3 %collective-permute-done.1.other_ref = f32[640,128]{1,0:T(8,128)S(1)} collective-permute-done((f32[640,128]{1,0:T(8,128)S(1)}, f32[640,128]{1,0:T(8,128)S(1)}, u32[]{:S(2)}, u32[]{:S(2)}) %collective-permute-start.1) | collective-permute-done | bytes 327712 | tf_op jit(solution)/shard_map/ppermute | solution.py:200
  54.2 0.0 copy-done.1
  54.2 0.0 copy-done.2
  54.2 16.7 %shard_map.42 = (f32[2048,256]{1,0:T(8,128)}, f32[256,512]{1,0:T(8,128)}) custom-call(f32[640,128]{1,0:T(8,128)S(1)} %bitcast.3, f32[640,128]{1,0:T(8,128)S(1)} %collective-permute-done.1.other_ref, bf16[512,256]{1,0:T(8,128)(2,1)S(1)} %copy-done.2, bf16[2048,512]{1,0:T(8,128)(2,1)S(1)} %copy-done.1), custom_call_target="tpu_custom_call" | custom-call | tf_op jit(solution)/shard_map/pallas_call | solution.py:165
  (5 shorter events, 0.1 us)
Async XLA Ops:
  0.6 1.6 %copy-start = (bf16[2048,512]{1,0:T(8,128)(2,1)S(1)}, bf16[2048,512]{1,0:T(8,128)(2,1)}, u32[]{:S(2)}) copy-start(bf16[2048,512]{1,0:T(8,128)(2,1)} %table_hbm.1) | copy-start | bytes 6291460
  3.3 50.9 %copy-start.1 = (bf16[2048,512]{1,0:T(8,128)(2,1)S(1)}, bf16[2048,512]{1,0:T(8,128)(2,1)}, u32[]{:S(2)}) copy-start(bf16[2048,512]{1,0:T(8,128)(2,1)} %table_hbm.1) | copy-start | bytes 6291460
  3.3 50.9 %copy-start.2 = (bf16[512,256]{1,0:T(8,128)(2,1)S(1)}, bf16[512,256]{1,0:T(8,128)(2,1)}, u32[]{:S(2)}) copy-start(bf16[512,256]{1,0:T(8,128)(2,1)} %sketch_ref.1) | copy-start | bytes 786436
  3.3 4.6 %collective-permute-start = (f32[640,128]{1,0:T(8,128)S(1)}, f32[640,128]{1,0:T(8,128)S(1)}, u32[]{:S(2)}, u32[]{:S(2)}) collective-permute-start(f32[640,128]{1,0:T(8,128)S(1)} %get-tuple-element.5), channel_id=1, source_target_pairs={{0,4},{4,0},{1,5},{5,1},{2,6},{6,2},{3,7},{7,3},{8,12},{12,8},{9,1... | collective-permute-start | bytes 983048 | tf_op jit(solution)/shard_map/ppermute | solution.py:196
  48.6 5.6 %collective-permute-start.1 = (f32[640,128]{1,0:T(8,128)S(1)}, f32[640,128]{1,0:T(8,128)S(1)}, u32[]{:S(2)}, u32[]{:S(2)}) collective-permute-start(f32[640,128]{1,0:T(8,128)S(1)} %bitcast.2), channel_id=1, source_target_pairs={{0,4},{4,0},{1,5},{5,1},{2,6},{6,2},{3,7},{7,3},{8,12},{12,8},{9,1... | collective-permute-start | bytes 983048 | tf_op jit(solution)/shard_map/ppermute | solution.py:200

commit v4 on v3

--- a/solution.py
+++ b/solution.py
@@ -51,7 +51,7 @@
     return jnp.concatenate(out, 0)
 
 
-def inverse_root(gram):
+def root_factors(gram):
     n = gram.shape[0]
     eye = lax.broadcasted_iota(jnp.int32, (n, n), 0) == lax.broadcasted_iota(jnp.int32, (n, n), 1)
     parts = split(gram)
@@ -73,48 +73,45 @@
         square = product(parts, parts, False)
         z = z + product(split(z), parts, False)
         e = 1.5 * square + product(split(square), parts, False)
-    z = z + product(split(z), split(e), False)
-    return z * (1.0 / jnp.sqrt(scale))
-
-
-def gram_kernel(table_ref, keep_ref, send_ref):
-    table = table_ref[...]
-    k = table.shape[1] // 2
-
-    def gram(a, b):
-        return lax.dot_general(a, b, (((0,), (0,)), ((), ())), preferred_element_type=F32)
-
-    upper = gram(table[:, :k], table)
-    lower = gram(table[:, k:], table[:, k:])
-    tiles = []
-    for i, j in PAIRS:
-        source, row, col = (upper, i, j) if i < 2 else (lower, i - 2, j - 2)
-        tiles.append(source[row * TILE : (row + 1) * TILE, col * TILE : (col + 1) * TILE])
-    count = len(PAIRS) // 2
+    return z * (1.0 / jnp.sqrt(scale)), e
+
+
+def last_sweep(a, parts):
+    return a + product(split(a), parts, False)
+
+
+def half_gram_kernel(mine, table_ref, half_ref):
     core = lax.axis_index("core")
 
-    def store(mine, others):
-        for n in range(count):
-            rows = pl.ds(n * TILE, TILE)
-            keep_ref[rows, :] = mine[n]
-            send_ref[rows, :] = others[n]
-
-    @pl.when(core == 0)
+    def tiles(*blocks):
+        row = 0
+        for rows, cols in blocks:
+            gram = lax.dot_general(
+                table_ref[:, rows], table_ref[:, cols], (((0,), (0,)), ((), ())), preferred_element_type=F32
+            )
+            for i in range(0, gram.shape[0], TILE):
+                for j in range(0, gram.shape[1], TILE):
+                    half_ref[row : row + TILE, :] = gram[i : i + TILE, j : j + TILE]
+                    row += TILE
+
+    def cols(first, last):
+        return slice(first * TILE, last * TILE)
+
+    @pl.when((core == 0) == mine)
     def _():
-        store(tiles[:count], tiles[count:])
-
-    @pl.when(core != 0)
+        tiles((cols(0, 1), cols(0, 4)), (cols(1, 2), cols(1, 2)))
+
+    @pl.when((core == 0) != mine)
     def _():
-        store(tiles[count:], tiles[:count])
-
-
-def gram_call(table):
-    half = jax.ShapeDtypeStruct((HALF, TILE), F32)
+        tiles((cols(1, 3), cols(2, 4)), (cols(3, 4), cols(3, 4)))
+
+
+def half_gram(table, mine):
     return pl.pallas_call(
-        gram_kernel,
-        out_shape=(half, half),
+        functools.partial(half_gram_kernel, mine),
+        out_shape=jax.ShapeDtypeStruct((HALF, TILE), F32),
         in_specs=[VMEM],
-        out_specs=(VMEM, VMEM),
+        out_specs=VMEM,
         compiler_params=PARAMS,
     )(table)
 
@@ -136,11 +133,14 @@
     sketch = sketch_ref[...]
     first = split(product(total, (sketch,), True))
     sketch_t = sketch.astype(F32).T.astype(BF16)
-    power = product(first, split(inverse_root(product((sketch_t,), first, True))), True)
+    z, e = root_factors(product((sketch_t,), first, True))
+    power = last_sweep(product(first, split(z), True), split(e))
     parts = split(power)
     table_power = split(product(total, parts, True))
-    second_inverse = split(inverse_root(product(split(power.T), table_power, True)))
-    weight = split(product(parts, second_inverse, True) * size)
+    z, e = root_factors(product(split(power.T), table_power, True))
+    z_parts, e_parts = split(z), split(e)
+    weight = split(last_sweep(product(parts, z_parts, True), e_parts) * size)
+    second_inverse = split(z + product(z_parts, e_parts, False))
     fetch.wait()
     copies = []
     blocks = table.shape[0] // BLOCK
@@ -150,7 +150,7 @@
         copy = pltpu.make_async_copy(basis.at[rows], basis_hbm.at[rows], out_sem.at[index])
         copy.start()
         copies.append(copy)
-        if index == 0:
+        if index == 1:
             coeff[...] = product(table_power, second_inverse, True).T * (1.0 / size)
             copy = pltpu.make_async_copy(coeff, coeff_hbm, out_sem.at[blocks])
             copy.start()
@@ -192,8 +192,8 @@
     count = table.shape[0] * lax.axis_size(("x", "z", "core", "y"))
     plane = ("x", "y")
     swap = [(0, 1), (1, 0)]
-    keep, send = gram_call(table)
-    half = keep + lax.ppermute(send, "core", swap)
+    sent = lax.ppermute(half_gram(table, False), "core", swap)
+    half = half_gram(table, True) + sent
     part = scatter_sum(half.reshape(lax.axis_size(plane), -1, TILE), plane)
     part = jnp.sum(gather(part, "z"), 0)
     mine = gather(part, plane).reshape(HALF, TILE)

time: 71.3 us -> 70.6 us (level)
  transfers between devices with their start and end apart: 2 -> 2, of which waited for: 2 -> 2; matrix products, arithmetic and copies ran while one was open for 0% -> 0% of each run, Pallas kernels for 0% -> 1%
where the time goes in v4:
time: 70.6 us; the launch traced here: 70.4 us
  blocking collectives  41 us (58%)
  Pallas kernels  17.6 us (25%)
  starting transfers between devices  7.37 us (10%)
  waiting for transfers between devices  1.87 us (3%)
  local copies, waits for them, and re-layouts  1.64 us (2%)
  between operations  0.86 us (1%)
    all_to_all x2, blocking collectives, gather(): return lax.all_to_all(copies, axes, 0, 0)  28.1 us
    pallas_call x1, Pallas kernels, finish_call(): pl.pallas_call(functools.partial(finish, size), out_shape=(jax.ShapeDtype...  16.4 us
    all_to_all x1, blocking collectives, scatter_sum(): return jnp.sum(lax.all_to_all(block, axes, 0, 0), 0)  12.9 us
    ppermute x1, starting transfers between devices, on_device(): other = lax.ppermute(mine, 'core', swap)  4.03 us
    ppermute x1, starting transfers between devices, on_device(): sent = lax.ppermute(half_gram(table, False), 'core', swap)  3.33 us
    unnamed x6, local copies, waits for them, and re-layouts  1.6 us
  transfers between devices with their start and end apart: 2, of which 2 were waited for; matrix products, arithmetic and copies ran while one was open for 0% of the time, Pallas kernels for 1%

profile of v4, /device:TPU:1, one launch (start us, length us, event | category | flops | bytes accessed | tf_op | source)
XLA Modules:
  0.0 70.4 jit_solution(7851891627880154632)
XLA Ops:
  0.6 0.0 copy-start
  0.6 1.6 %copy-done = bf16[2048,512]{1,0:T(8,128)(2,1)S(1)} copy-done((bf16[2048,512]{1,0:T(8,128)(2,1)S(1)}, bf16[2048,512]{1,0:T(8,128)(2,1)}, u32[]{:S(2)}) %copy-start) | copy-done | bytes 2097176
  2.2 0.6 shard_map.42
  2.8 3.3 %collective-permute-start = (f32[640,128]{1,0:T(8,128)S(1)}, f32[640,128]{1,0:T(8,128)S(1)}, u32[]{:S(2)}, u32[]{:S(2)}) collective-permute-start(f32[640,128]{1,0:T(8,128)S(1)} %shard_map.42), channel_id=1, source_target_pairs={{0,4},{4,0},{1,5},{5,1},{2,6},{6,2},{3,7},{7,3},{8,12},{12,8},{9,1... | collective-permute-start | bytes 983048 | tf_op jit(solution)/shard_map/ppermute | solution.py:195
  6.2 0.6 shard_map.41
  6.8 0.0 copy-start.1
  6.8 0.0 copy-start.2
  6.8 0.6 collective-permute-done
  7.5 12.9 %all_to_all.15 = f32[16,40,128]{2,1,0:T(8,128)S(1)} all-to-all(f32[16,40,128]{2,1,0:T(8,128)S(1)} %bitcast.4), channel_id=1, replica_groups=mesh['x'=4,'z'=8,'core'=2,'y'=4] {'x','y'}, dimensions={0} | all-to-all | bytes 655360 | tf_op jit(solution)/shard_map/all_to_all | solution.py:182
  20.4 16.4 %all_to_all.16 = f32[8,40,128]{2,1,0:T(8,128)S(1)} all-to-all(f32[8,40,128]{2,1,0:T(8,128)S(1)} %broadcast_in_dim.4), channel_id=1, replica_groups=mesh['x'=4,'z'=8,'core'=2,'y'=4] {'z'}, dimensions={0} | all-to-all | bytes 327680 | tf_op jit(solution)/shard_map/all_to_all | solution.py:188
  36.8 11.7 %all_to_all.17 = f32[16,40,128]{2,1,0:T(8,128)S(1)} all-to-all(f32[16,40,128]{2,1,0:T(8,128)S(1)} %broadcast_in_dim.5), channel_id=1, replica_groups=mesh['x'=4,'z'=8,'core'=2,'y'=4] {'x','y'}, dimensions={0} | all-to-all | bytes 655360 | tf_op jit(solution)/shard_map/all_to_all | solution.py:188
  48.6 4.0 %collective-permute-start.1 = (f32[640,128]{1,0:T(8,128)S(1)}, f32[640,128]{1,0:T(8,128)S(1)}, u32[]{:S(2)}, u32[]{:S(2)}) collective-permute-start(f32[640,128]{1,0:T(8,128)S(1)} %bitcast.2), channel_id=1, source_target_pairs={{0,4},{4,0},{1,5},{5,1},{2,6},{6,2},{3,7},{7,3},{8,12},{12,8},{9,1... | collective-permute-start | bytes 983048 | tf_op jit(solution)/shard_map/ppermute | solution.py:200
  52.6 1.3 %collective-permute-done.1.other_ref = f32[640,128]{1,0:T(8,128)S(1)} collective-permute-done((f32[640,128]{1,0:T(8,128)S(1)}, f32[640,128]{1,0:T(8,128)S(1)}, u32[]{:S(2)}, u32[]{:S(2)}) %collective-permute-start.1) | collective-permute-done | bytes 327712 | tf_op jit(solution)/shard_map/ppermute | solution.py:200
  53.9 0.0 copy-done.1
  53.9 0.0 copy-done.2
  53.9 16.4 %shard_map.43 = (f32[2048,256]{1,0:T(8,128)}, f32[256,512]{1,0:T(8,128)}) custom-call(f32[640,128]{1,0:T(8,128)S(1)} %bitcast.3, f32[640,128]{1,0:T(8,128)S(1)} %collective-permute-done.1.other_ref, bf16[512,256]{1,0:T(8,128)(2,1)S(1)} %copy-done.2, bf16[2048,512]{1,0:T(8,128)(2,1)S(1)} %copy-done.1), custom_call_target="tpu_custom_call" | custom-call | tf_op jit(solution)/shard_map/pallas_call | solution.py:165
  (5 shorter events, 0.1 us)
Async XLA Ops:
  0.6 1.6 %copy-start = (bf16[2048,512]{1,0:T(8,128)(2,1)S(1)}, bf16[2048,512]{1,0:T(8,128)(2,1)}, u32[]{:S(2)}) copy-start(bf16[2048,512]{1,0:T(8,128)(2,1)} %table_hbm.1) | copy-start | bytes 6291460
  2.8 4.6 %collective-permute-start = (f32[640,128]{1,0:T(8,128)S(1)}, f32[640,128]{1,0:T(8,128)S(1)}, u32[]{:S(2)}, u32[]{:S(2)}) collective-permute-start(f32[640,128]{1,0:T(8,128)S(1)} %shard_map.42), channel_id=1, source_target_pairs={{0,4},{4,0},{1,5},{5,1},{2,6},{6,2},{3,7},{7,3},{8,12},{12,8},{9,1... | collective-permute-start | bytes 983048 | tf_op jit(solution)/shard_map/ppermute | solution.py:195
  6.8 47.1 %copy-start.1 = (bf16[2048,512]{1,0:T(8,128)(2,1)S(1)}, bf16[2048,512]{1,0:T(8,128)(2,1)}, u32[]{:S(2)}) copy-start(bf16[2048,512]{1,0:T(8,128)(2,1)} %table_hbm.1) | copy-start | bytes 6291460
  6.8 47.1 %copy-start.2 = (bf16[512,256]{1,0:T(8,128)(2,1)S(1)}, bf16[512,256]{1,0:T(8,128)(2,1)}, u32[]{:S(2)}) copy-start(bf16[512,256]{1,0:T(8,128)(2,1)} %sketch_ref.1) | copy-start | bytes 786436
  48.6 5.3 %collective-permute-start.1 = (f32[640,128]{1,0:T(8,128)S(1)}, f32[640,128]{1,0:T(8,128)S(1)}, u32[]{:S(2)}, u32[]{:S(2)}) collective-permute-start(f32[640,128]{1,0:T(8,128)S(1)} %bitcast.2), channel_id=1, source_target_pairs={{0,4},{4,0},{1,5},{5,1},{2,6},{6,2},{3,7},{7,3},{8,12},{12,8},{9,1... | collective-permute-start | bytes 983048 | tf_op jit(solution)/shard_map/ppermute | solution.py:200

commit v5 on v4

--- a/solution.py
+++ b/solution.py
@@ -195,7 +195,8 @@
     sent = lax.ppermute(half_gram(table, False), "core", swap)
     half = half_gram(table, True) + sent
     part = scatter_sum(half.reshape(lax.axis_size(plane), -1, TILE), plane)
-    part = jnp.sum(gather(part, "z"), 0)
+    for apart in (4, 1, 2):
+        part = part + lax.ppermute(part, "z", [(i, i ^ apart) for i in range(lax.axis_size("z"))])
     mine = gather(part, plane).reshape(HALF, TILE)
     other = lax.ppermute(mine, "core", swap)
     return finish_call(math.sqrt(count), mine, other, sketch, table)

time: 70.6 us -> 70.4 us (level)
  blocking collectives: 41 us -> 24.6 us
  starting transfers between devices: 7.37 us -> 18.6 us
  waiting for transfers between devices: 1.87 us -> 6.86 us
    all_to_all x2 -> x1, blocking collectives: 28.1 us -> 11.7 us  [gather(): return lax.all_to_all(copies, axes, 0, 0)]
    ppermute x0 -> x3, starting transfers between devices: none -> 9.46 us  [on_device(): lax.ppermute(part, 'z', [(i, i ^ apart) for i in range(lax.axis_size('z'))])]
    ppermute x0 -> x3, waiting for transfers between devices: none -> 4.99 us  [on_device(): lax.ppermute(part, 'z', [(i, i ^ apart) for i in range(lax.axis_size('z'))])]
    ppermute x1, starting transfers between devices: 4.03 us -> 5.83 us  [on_device(): other = lax.ppermute(mine, 'core', swap)]
  transfers between devices with their start and end apart: 2 -> 5, of which waited for: 2 -> 5; matrix products, arithmetic and copies ran while one was open for 0% -> 0% of each run, Pallas kernels for 1% -> 1%
where the time goes in v5:
time: 70.4 us; the launch traced here: 70.2 us
  blocking collectives  24.6 us (35%)
  starting transfers between devices  18.6 us (26%)
  Pallas kernels  17.6 us (25%)
  waiting for transfers between devices  6.86 us (10%)
  local copies, waits for them, and re-layouts  1.62 us (2%)
  between operations  0.85 us (1%)
    pallas_call x1, Pallas kernels, finish_call(): pl.pallas_call(functools.partial(finish, size), out_shape=(jax.ShapeDtype...  16.4 us
    all_to_all x1, blocking collectives, scatter_sum(): return jnp.sum(lax.all_to_all(block, axes, 0, 0), 0)  12.9 us
    all_to_all x1, blocking collectives, gather(): return lax.all_to_all(copies, axes, 0, 0)  11.7 us
    ppermute x3, starting transfers between devices, on_device(): lax.ppermute(part, 'z', [(i, i ^ apart) for i in range(lax.axis_size('z'))])  9.46 us
    ppermute x1, starting transfers between devices, on_device(): other = lax.ppermute(mine, 'core', swap)  5.83 us
    ppermute x3, waiting for transfers between devices, on_device(): lax.ppermute(part, 'z', [(i, i ^ apart) for i in range(lax.axis_size('z'))])  4.99 us
    ppermute x1, starting transfers between devices, on_device(): sent = lax.ppermute(half_gram(table, False), 'core', swap)  3.33 us
    unnamed x6, local copies, waits for them, and re-layouts  1.6 us
  transfers between devices with their start and end apart: 5, of which 5 were waited for; matrix products, arithmetic and copies ran while one was open for 0% of the time, Pallas kernels for 1%

profile of v5, /device:TPU:1, one launch (start us, length us, event | category | flops | bytes accessed | tf_op | source)
XLA Modules:
  0.0 70.2 jit_solution(11479360902986683938)
XLA Ops:
  0.6 0.0 copy-start
  0.6 1.6 %copy-done = bf16[2048,512]{1,0:T(8,128)(2,1)S(1)} copy-done((bf16[2048,512]{1,0:T(8,128)(2,1)S(1)}, bf16[2048,512]{1,0:T(8,128)(2,1)}, u32[]{:S(2)}) %copy-start) | copy-done | bytes 2097176
  2.2 0.6 shard_map.42
  2.8 3.3 %collective-permute-start = (f32[640,128]{1,0:T(8,128)S(1)}, f32[640,128]{1,0:T(8,128)S(1)}, u32[]{:S(2)}, u32[]{:S(2)}) collective-permute-start(f32[640,128]{1,0:T(8,128)S(1)} %shard_map.42), channel_id=1, source_target_pairs={{0,4},{4,0},{1,5},{5,1},{2,6},{6,2},{3,7},{7,3},{8,12},{12,8},{9,1... | collective-permute-start | bytes 983048 | tf_op jit(solution)/shard_map/ppermute | solution.py:195
  6.2 0.6 shard_map.41
  6.8 0.0 copy-start.1
  6.8 0.0 copy-start.2
  6.8 0.6 collective-permute-done
  7.5 12.9 %all_to_all.10 = f32[16,40,128]{2,1,0:T(8,128)S(1)} all-to-all(f32[16,40,128]{2,1,0:T(8,128)S(1)} %bitcast.4), channel_id=1, replica_groups=mesh['x'=4,'z'=8,'core'=2,'y'=4] {'x','y'}, dimensions={0} | all-to-all | bytes 655360 | tf_op jit(solution)/shard_map/all_to_all | solution.py:182
  20.4 7.0 %collective-permute-start.1 = (f32[40,128]{1,0:T(8,128)S(1)}, f32[40,128]{1,0:T(8,128)S(1)}, u32[]{:S(2)}, u32[]{:S(2)}) collective-permute-start(f32[40,128]{1,0:T(8,128)S(1)} %reduce_sum.9), channel_id=1, source_target_pairs={{0,32},{8,40},{16,48},{24,56},{32,0},{40,8},{48,16},{56,24},{1,33}... | collective-permute-start | bytes 61448 | tf_op jit(solution)/shard_map/ppermute | solution.py:199
  27.4 1.2 %collective-permute-done.1 = f32[40,128]{1,0:T(8,128)S(1)} collective-permute-done((f32[40,128]{1,0:T(8,128)S(1)}, f32[40,128]{1,0:T(8,128)S(1)}, u32[]{:S(2)}, u32[]{:S(2)}) %collective-permute-start.1) | collective-permute-done | bytes 20512 | tf_op jit(solution)/shard_map/ppermute | solution.py:199
  28.6 0.7 %collective-permute-start.2 = (f32[40,128]{1,0:T(8,128)S(1)}, f32[40,128]{1,0:T(8,128)S(1)}, u32[]{:S(2)}, u32[]{:S(2)}) collective-permute-start(f32[40,128]{1,0:T(8,128)S(1)} %add.13), channel_id=1, source_target_pairs={{0,8},{8,0},{16,24},{24,16},{32,40},{40,32},{48,56},{56,48},{1,9},... | collective-permute-start | bytes 61448 | tf_op jit(solution)/shard_map/ppermute | solution.py:199
  29.3 1.9 %collective-permute-done.2 = f32[40,128]{1,0:T(8,128)S(1)} collective-permute-done((f32[40,128]{1,0:T(8,128)S(1)}, f32[40,128]{1,0:T(8,128)S(1)}, u32[]{:S(2)}, u32[]{:S(2)}) %collective-permute-start.2) | collective-permute-done | bytes 20512 | tf_op jit(solution)/shard_map/ppermute | solution.py:199
  31.2 1.7 %collective-permute-start.3 = (f32[40,128]{1,0:T(8,128)S(1)}, f32[40,128]{1,0:T(8,128)S(1)}, u32[]{:S(2)}, u32[]{:S(2)}) collective-permute-start(f32[40,128]{1,0:T(8,128)S(1)} %add.14), channel_id=1, source_target_pairs={{0,16},{8,24},{16,0},{24,8},{32,48},{40,56},{48,32},{56,40},{1,17}... | collective-permute-start | bytes 61448 | tf_op jit(solution)/shard_map/ppermute | solution.py:199
  32.9 1.9 %collective-permute-done.3 = f32[40,128]{1,0:T(8,128)S(1)} collective-permute-done((f32[40,128]{1,0:T(8,128)S(1)}, f32[40,128]{1,0:T(8,128)S(1)}, u32[]{:S(2)}, u32[]{:S(2)}) %collective-permute-start.3) | collective-permute-done | bytes 20512 | tf_op jit(solution)/shard_map/ppermute | solution.py:199
  34.9 11.7 %all_to_all.11 = f32[16,40,128]{2,1,0:T(8,128)S(1)} all-to-all(f32[16,40,128]{2,1,0:T(8,128)S(1)} %broadcast_in_dim.2), channel_id=1, replica_groups=mesh['x'=4,'z'=8,'core'=2,'y'=4] {'x','y'}, dimensions={0} | all-to-all | bytes 655360 | tf_op jit(solution)/shard_map/all_to_all | solution.py:188
  46.6 5.8 %collective-permute-start.4 = (f32[640,128]{1,0:T(8,128)S(1)}, f32[640,128]{1,0:T(8,128)S(1)}, u32[]{:S(2)}, u32[]{:S(2)}) collective-permute-start(f32[640,128]{1,0:T(8,128)S(1)} %bitcast.2), channel_id=1, source_target_pairs={{0,4},{4,0},{1,5},{5,1},{2,6},{6,2},{3,7},{7,3},{8,12},{12,8},{9,1... | collective-permute-start | bytes 983048 | tf_op jit(solution)/shard_map/ppermute | solution.py:201
  52.4 1.3 %collective-permute-done.4.other_ref = f32[640,128]{1,0:T(8,128)S(1)} collective-permute-done((f32[640,128]{1,0:T(8,128)S(1)}, f32[640,128]{1,0:T(8,128)S(1)}, u32[]{:S(2)}, u32[]{:S(2)}) %collective-permute-start.4) | collective-permute-done | bytes 327712 | tf_op jit(solution)/shard_map/ppermute | solution.py:201
  53.7 0.0 copy-done.1
  53.7 0.0 copy-done.2
  53.7 16.4 %shard_map.43 = (f32[2048,256]{1,0:T(8,128)}, f32[256,512]{1,0:T(8,128)}) custom-call(f32[640,128]{1,0:T(8,128)S(1)} %bitcast.3, f32[640,128]{1,0:T(8,128)S(1)} %collective-permute-done.4.other_ref, bf16[512,256]{1,0:T(8,128)(2,1)S(1)} %copy-done.2, bf16[2048,512]{1,0:T(8,128)(2,1)S(1)} %copy-done.1), custom_call_target="tpu_custom_call" | custom-call | tf_op jit(solution)/shard_map/pallas_call | solution.py:165
  (6 shorter events, 0.1 us)
Async XLA Ops:
  0.6 1.6 %copy-start = (bf16[2048,512]{1,0:T(8,128)(2,1)S(1)}, bf16[2048,512]{1,0:T(8,128)(2,1)}, u32[]{:S(2)}) copy-start(bf16[2048,512]{1,0:T(8,128)(2,1)} %table_hbm.1) | copy-start | bytes 6291460
  2.8 4.6 %collective-permute-start = (f32[640,128]{1,0:T(8,128)S(1)}, f32[640,128]{1,0:T(8,128)S(1)}, u32[]{:S(2)}, u32[]{:S(2)}) collective-permute-start(f32[640,128]{1,0:T(8,128)S(1)} %shard_map.42), channel_id=1, source_target_pairs={{0,4},{4,0},{1,5},{5,1},{2,6},{6,2},{3,7},{7,3},{8,12},{12,8},{9,1... | collective-permute-start | bytes 983048 | tf_op jit(solution)/shard_map/ppermute | solution.py:195
  6.8 46.9 %copy-start.1 = (bf16[2048,512]{1,0:T(8,128)(2,1)S(1)}, bf16[2048,512]{1,0:T(8,128)(2,1)}, u32[]{:S(2)}) copy-start(bf16[2048,512]{1,0:T(8,128)(2,1)} %table_hbm.1) | copy-start | bytes 6291460
  6.8 46.9 %copy-start.2 = (bf16[512,256]{1,0:T(8,128)(2,1)S(1)}, bf16[512,256]{1,0:T(8,128)(2,1)}, u32[]{:S(2)}) copy-start(bf16[512,256]{1,0:T(8,128)(2,1)} %sketch_ref.1) | copy-start | bytes 786436
  20.4 8.2 %collective-permute-start.1 = (f32[40,128]{1,0:T(8,128)S(1)}, f32[40,128]{1,0:T(8,128)S(1)}, u32[]{:S(2)}, u32[]{:S(2)}) collective-permute-start(f32[40,128]{1,0:T(8,128)S(1)} %reduce_sum.9), channel_id=1, source_target_pairs={{0,32},{8,40},{16,48},{24,56},{32,0},{40,8},{48,16},{56,24},{1,33}... | collective-permute-start | bytes 61448 | tf_op jit(solution)/shard_map/ppermute | solution.py:199
  28.6 2.6 %collective-permute-start.2 = (f32[40,128]{1,0:T(8,128)S(1)}, f32[40,128]{1,0:T(8,128)S(1)}, u32[]{:S(2)}, u32[]{:S(2)}) collective-permute-start(f32[40,128]{1,0:T(8,128)S(1)} %add.13), channel_id=1, source_target_pairs={{0,8},{8,0},{16,24},{24,16},{32,40},{40,32},{48,56},{56,48},{1,9},... | collective-permute-start | bytes 61448 | tf_op jit(solution)/shard_map/ppermute | solution.py:199
  31.2 3.6 %collective-permute-start.3 = (f32[40,128]{1,0:T(8,128)S(1)}, f32[40,128]{1,0:T(8,128)S(1)}, u32[]{:S(2)}, u32[]{:S(2)}) collective-permute-start(f32[40,128]{1,0:T(8,128)S(1)} %add.14), channel_id=1, source_target_pairs={{0,16},{8,24},{16,0},{24,8},{32,48},{40,56},{48,32},{56,40},{1,17}... | collective-permute-start | bytes 61448 | tf_op jit(solution)/shard_map/ppermute | solution.py:199
  46.6 7.1 %collective-permute-start.4 = (f32[640,128]{1,0:T(8,128)S(1)}, f32[640,128]{1,0:T(8,128)S(1)}, u32[]{:S(2)}, u32[]{:S(2)}) collective-permute-start(f32[640,128]{1,0:T(8,128)S(1)} %bitcast.2), channel_id=1, source_target_pairs={{0,4},{4,0},{1,5},{5,1},{2,6},{6,2},{3,7},{7,3},{8,12},{12,8},{9,1... | collective-permute-start | bytes 983048 | tf_op jit(solution)/shard_map/ppermute | solution.py:201

commit v6 on v5

--- a/solution.py
+++ b/solution.py
@@ -116,9 +116,7 @@
     )(table)
 
 
-def finish(size, mine_ref, other_ref, sketch_ref, table_hbm, basis_hbm, coeff_hbm, table, basis, coeff, in_sem, out_sem):
-    fetch = pltpu.make_async_copy(table_hbm, table, in_sem)
-    fetch.start()
+def finish(size, mine_ref, other_ref, sketch_ref, table, basis_hbm, coeff_hbm, basis, coeff, out_sem):
     first_core = lax.axis_index("core") == 0
     mine, other = mine_ref[...], other_ref[...]
     tiles = {}
@@ -141,7 +139,6 @@
     z_parts, e_parts = split(z), split(e)
     weight = split(last_sweep(product(parts, z_parts, True), e_parts) * size)
     second_inverse = split(z + product(z_parts, e_parts, False))
-    fetch.wait()
     copies = []
     blocks = table.shape[0] // BLOCK
     for index in range(blocks):
@@ -165,13 +162,11 @@
     return pl.pallas_call(
         functools.partial(finish, size),
         out_shape=(jax.ShapeDtypeStruct((rows, k), F32), jax.ShapeDtypeStruct((k, n), F32)),
-        in_specs=[VMEM, VMEM, VMEM, HBM],
+        in_specs=[VMEM, VMEM, VMEM, VMEM],
         out_specs=(HBM, HBM),
         scratch_shapes=[
-            pltpu.VMEM((rows, n), BF16),
             pltpu.VMEM((rows, k), F32),
             pltpu.VMEM((k, n), F32),
-            pltpu.SemaphoreType.DMA,
             pltpu.SemaphoreType.DMA((rows // BLOCK + 1,)),
         ],
         compiler_params=PARAMS,

time: 70.4 us -> 70.1 us (level)
  no operation moved by 1% of the time
where the time goes in v6:
time: 70.1 us; the launch traced here: 69.9 us
  blocking collectives  24.6 us (35%)
  starting transfers between devices  18.6 us (27%)
  Pallas kernels  17.3 us (25%)
  waiting for transfers between devices  6.86 us (10%)
  local copies, waits for them, and re-layouts  1.62 us (2%)
  between operations  0.85 us (1%)
    pallas_call x1, Pallas kernels, finish_call(): pl.pallas_call(functools.partial(finish, size), out_shape=(jax.ShapeDtype...  16.1 us
    all_to_all x1, blocking collectives, scatter_sum(): return jnp.sum(lax.all_to_all(block, axes, 0, 0), 0)  12.9 us
    all_to_all x1, blocking collectives, gather(): return lax.all_to_all(copies, axes, 0, 0)  11.7 us
    ppermute x3, starting transfers between devices, on_device(): lax.ppermute(part, 'z', [(i, i ^ apart) for i in range(lax.axis_size('z'))])  9.46 us
    ppermute x1, starting transfers between devices, on_device(): other = lax.ppermute(mine, 'core', swap)  5.83 us
    ppermute x3, waiting for transfers between devices, on_device(): lax.ppermute(part, 'z', [(i, i ^ apart) for i in range(lax.axis_size('z'))])  4.99 us
    ppermute x1, starting transfers between devices, on_device(): sent = lax.ppermute(half_gram(table, False), 'core', swap)  3.33 us
    unnamed x6, local copies, waits for them, and re-layouts  1.6 us
  transfers between devices with their start and end apart: 5, of which 5 were waited for; matrix products, arithmetic and copies ran while one was open for 0% of the time, Pallas kernels for 1%

profile of v6, /device:TPU:1, one launch (start us, length us, event | category | flops | bytes accessed | tf_op | source)
XLA Modules:
  0.0 69.9 jit_solution(9462557909474821416)
XLA Ops:
  0.6 0.0 copy-start
  0.6 1.6 %copy-done = bf16[2048,512]{1,0:T(8,128)(2,1)S(1)} copy-done((bf16[2048,512]{1,0:T(8,128)(2,1)S(1)}, bf16[2048,512]{1,0:T(8,128)(2,1)}, u32[]{:S(2)}) %copy-start) | copy-done | bytes 2097176
  2.2 0.6 shard_map.42
  2.8 3.3 %collective-permute-start = (f32[640,128]{1,0:T(8,128)S(1)}, f32[640,128]{1,0:T(8,128)S(1)}, u32[]{:S(2)}, u32[]{:S(2)}) collective-permute-start(f32[640,128]{1,0:T(8,128)S(1)} %shard_map.42), channel_id=1, source_target_pairs={{0,4},{4,0},{1,5},{5,1},{2,6},{6,2},{3,7},{7,3},{8,12},{12,8},{9,1... | collective-permute-start | bytes 983048 | tf_op jit(solution)/shard_map/ppermute | solution.py:190
  6.2 0.6 shard_map.41
  6.8 0.0 copy-start.1
  6.8 0.0 copy-start.2
  6.8 0.6 collective-permute-done
  7.5 12.9 %all_to_all.10 = f32[16,40,128]{2,1,0:T(8,128)S(1)} all-to-all(f32[16,40,128]{2,1,0:T(8,128)S(1)} %bitcast.4), channel_id=1, replica_groups=mesh['x'=4,'z'=8,'core'=2,'y'=4] {'x','y'}, dimensions={0} | all-to-all | bytes 655360 | tf_op jit(solution)/shard_map/all_to_all | solution.py:177
  20.4 7.0 %collective-permute-start.1 = (f32[40,128]{1,0:T(8,128)S(1)}, f32[40,128]{1,0:T(8,128)S(1)}, u32[]{:S(2)}, u32[]{:S(2)}) collective-permute-start(f32[40,128]{1,0:T(8,128)S(1)} %reduce_sum.9), channel_id=1, source_target_pairs={{0,32},{8,40},{16,48},{24,56},{32,0},{40,8},{48,16},{56,24},{1,33}... | collective-permute-start | bytes 61448 | tf_op jit(solution)/shard_map/ppermute | solution.py:194
  27.4 1.2 %collective-permute-done.1 = f32[40,128]{1,0:T(8,128)S(1)} collective-permute-done((f32[40,128]{1,0:T(8,128)S(1)}, f32[40,128]{1,0:T(8,128)S(1)}, u32[]{:S(2)}, u32[]{:S(2)}) %collective-permute-start.1) | collective-permute-done | bytes 20512 | tf_op jit(solution)/shard_map/ppermute | solution.py:194
  28.6 0.7 %collective-permute-start.2 = (f32[40,128]{1,0:T(8,128)S(1)}, f32[40,128]{1,0:T(8,128)S(1)}, u32[]{:S(2)}, u32[]{:S(2)}) collective-permute-start(f32[40,128]{1,0:T(8,128)S(1)} %add.13), channel_id=1, source_target_pairs={{0,8},{8,0},{16,24},{24,16},{32,40},{40,32},{48,56},{56,48},{1,9},... | collective-permute-start | bytes 61448 | tf_op jit(solution)/shard_map/ppermute | solution.py:194
  29.3 1.9 %collective-permute-done.2 = f32[40,128]{1,0:T(8,128)S(1)} collective-permute-done((f32[40,128]{1,0:T(8,128)S(1)}, f32[40,128]{1,0:T(8,128)S(1)}, u32[]{:S(2)}, u32[]{:S(2)}) %collective-permute-start.2) | collective-permute-done | bytes 20512 | tf_op jit(solution)/shard_map/ppermute | solution.py:194
  31.2 1.7 %collective-permute-start.3 = (f32[40,128]{1,0:T(8,128)S(1)}, f32[40,128]{1,0:T(8,128)S(1)}, u32[]{:S(2)}, u32[]{:S(2)}) collective-permute-start(f32[40,128]{1,0:T(8,128)S(1)} %add.14), channel_id=1, source_target_pairs={{0,16},{8,24},{16,0},{24,8},{32,48},{40,56},{48,32},{56,40},{1,17}... | collective-permute-start | bytes 61448 | tf_op jit(solution)/shard_map/ppermute | solution.py:194
  32.9 1.9 %collective-permute-done.3 = f32[40,128]{1,0:T(8,128)S(1)} collective-permute-done((f32[40,128]{1,0:T(8,128)S(1)}, f32[40,128]{1,0:T(8,128)S(1)}, u32[]{:S(2)}, u32[]{:S(2)}) %collective-permute-start.3) | collective-permute-done | bytes 20512 | tf_op jit(solution)/shard_map/ppermute | solution.py:194
  34.9 11.7 %all_to_all.11 = f32[16,40,128]{2,1,0:T(8,128)S(1)} all-to-all(f32[16,40,128]{2,1,0:T(8,128)S(1)} %broadcast_in_dim.2), channel_id=1, replica_groups=mesh['x'=4,'z'=8,'core'=2,'y'=4] {'x','y'}, dimensions={0} | all-to-all | bytes 655360 | tf_op jit(solution)/shard_map/all_to_all | solution.py:183
  46.6 5.8 %collective-permute-start.4 = (f32[640,128]{1,0:T(8,128)S(1)}, f32[640,128]{1,0:T(8,128)S(1)}, u32[]{:S(2)}, u32[]{:S(2)}) collective-permute-start(f32[640,128]{1,0:T(8,128)S(1)} %bitcast.2), channel_id=1, source_target_pairs={{0,4},{4,0},{1,5},{5,1},{2,6},{6,2},{3,7},{7,3},{8,12},{12,8},{9,1... | collective-permute-start | bytes 983048 | tf_op jit(solution)/shard_map/ppermute | solution.py:196
  52.4 1.3 %collective-permute-done.4.other_ref = f32[640,128]{1,0:T(8,128)S(1)} collective-permute-done((f32[640,128]{1,0:T(8,128)S(1)}, f32[640,128]{1,0:T(8,128)S(1)}, u32[]{:S(2)}, u32[]{:S(2)}) %collective-permute-start.4) | collective-permute-done | bytes 327712 | tf_op jit(solution)/shard_map/ppermute | solution.py:196
  53.7 0.0 copy-done.1
  53.7 0.0 copy-done.2
  53.7 16.1 %shard_map.43 = (f32[2048,256]{1,0:T(8,128)}, f32[256,512]{1,0:T(8,128)}) custom-call(f32[640,128]{1,0:T(8,128)S(1)} %bitcast.3, f32[640,128]{1,0:T(8,128)S(1)} %collective-permute-done.4.other_ref, bf16[512,256]{1,0:T(8,128)(2,1)S(1)} %copy-done.2, bf16[2048,512]{1,0:T(8,128)(2,1)S(1)} %copy-done.1), custom_call_target="tpu_custom_call" | custom-call | tf_op jit(solution)/shard_map/pallas_call | solution.py:162
  (6 shorter events, 0.1 us)
Async XLA Ops:
  0.6 1.6 %copy-start = (bf16[2048,512]{1,0:T(8,128)(2,1)S(1)}, bf16[2048,512]{1,0:T(8,128)(2,1)}, u32[]{:S(2)}) copy-start(bf16[2048,512]{1,0:T(8,128)(2,1)} %table.1) | copy-start | bytes 6291460
  2.8 4.6 %collective-permute-start = (f32[640,128]{1,0:T(8,128)S(1)}, f32[640,128]{1,0:T(8,128)S(1)}, u32[]{:S(2)}, u32[]{:S(2)}) collective-permute-start(f32[640,128]{1,0:T(8,128)S(1)} %shard_map.42), channel_id=1, source_target_pairs={{0,4},{4,0},{1,5},{5,1},{2,6},{6,2},{3,7},{7,3},{8,12},{12,8},{9,1... | collective-permute-start | bytes 983048 | tf_op jit(solution)/shard_map/ppermute | solution.py:190
  6.8 46.9 %copy-start.1 = (bf16[2048,512]{1,0:T(8,128)(2,1)S(1)}, bf16[2048,512]{1,0:T(8,128)(2,1)}, u32[]{:S(2)}) copy-start(bf16[2048,512]{1,0:T(8,128)(2,1)} %table.1) | copy-start | bytes 6291460
  6.8 46.9 %copy-start.2 = (bf16[512,256]{1,0:T(8,128)(2,1)S(1)}, bf16[512,256]{1,0:T(8,128)(2,1)}, u32[]{:S(2)}) copy-start(bf16[512,256]{1,0:T(8,128)(2,1)} %sketch_ref.1) | copy-start | bytes 786436
  20.4 8.2 %collective-permute-start.1 = (f32[40,128]{1,0:T(8,128)S(1)}, f32[40,128]{1,0:T(8,128)S(1)}, u32[]{:S(2)}, u32[]{:S(2)}) collective-permute-start(f32[40,128]{1,0:T(8,128)S(1)} %reduce_sum.9), channel_id=1, source_target_pairs={{0,32},{8,40},{16,48},{24,56},{32,0},{40,8},{48,16},{56,24},{1,33}... | collective-permute-start | bytes 61448 | tf_op jit(solution)/shard_map/ppermute | solution.py:194
  28.6 2.6 %collective-permute-start.2 = (f32[40,128]{1,0:T(8,128)S(1)}, f32[40,128]{1,0:T(8,128)S(1)}, u32[]{:S(2)}, u32[]{:S(2)}) collective-permute-start(f32[40,128]{1,0:T(8,128)S(1)} %add.13), channel_id=1, source_target_pairs={{0,8},{8,0},{16,24},{24,16},{32,40},{40,32},{48,56},{56,48},{1,9},... | collective-permute-start | bytes 61448 | tf_op jit(solution)/shard_map/ppermute | solution.py:194
  31.2 3.6 %collective-permute-start.3 = (f32[40,128]{1,0:T(8,128)S(1)}, f32[40,128]{1,0:T(8,128)S(1)}, u32[]{:S(2)}, u32[]{:S(2)}) collective-permute-start(f32[40,128]{1,0:T(8,128)S(1)} %add.14), channel_id=1, source_target_pairs={{0,16},{8,24},{16,0},{24,8},{32,48},{40,56},{48,32},{56,40},{1,17}... | collective-permute-start | bytes 61448 | tf_op jit(solution)/shard_map/ppermute | solution.py:194
  46.6 7.1 %collective-permute-start.4 = (f32[640,128]{1,0:T(8,128)S(1)}, f32[640,128]{1,0:T(8,128)S(1)}, u32[]{:S(2)}, u32[]{:S(2)}) collective-permute-start(f32[640,128]{1,0:T(8,128)S(1)} %bitcast.2), channel_id=1, source_target_pairs={{0,4},{4,0},{1,5},{5,1},{2,6},{6,2},{3,7},{7,3},{8,12},{12,8},{9,1... | collective-permute-start | bytes 983048 | tf_op jit(solution)/shard_map/ppermute | solution.py:196
